TPU v7x, 128 devices: a whole 4x4x4 slice. The times are simulated.
128 devices in a mesh: labels: 32 (over z, y, core), queries: 4 (over x).
Axes of the slice: x: 4, y: 4, z: 4, core: 2. Of those that a mesh axis runs over, the one named last changes fastest.
Arguments:
- queries_in: bfloat16 [32768, 768], P(('queries', 'labels')), may hold values from -6 to 6
- classifier: bfloat16 [65536, 768], P('labels'), may hold values from -0.21875 to 0.21875
- owner_ids: int32 [32768, 8], P(('queries', 'labels')), may hold values from 0 to 31, all different within a row; in each aligned block of 256 rows (0 to 255, 256 to 511, ...) at most 128 rows name the same one
- local_ids: int32 [32768, 8], P(('queries', 'labels')), may hold values from 0 to 15
- targets: int32 [32768, 8, 128], P(('queries', 'labels')), may hold values 0 or 1
Outputs:
- query_loss: float32 [32768], P(('queries', 'labels'))
- feature_grad: float32 [32768, 768], P(('queries', 'labels'))
- weight_grad: bfloat16 [65536, 768], P(('labels', 'queries'))
Inputs may be any that keep to these rules, and one draw needn't show every extreme that they name: `owner_ids`: each row names 8 different owners. Among the rows of one device no owner is named by more than 128 rows, a bound that some block reaches.
All inputs are finite; a program needn't handle non-finite values. No bound on the sum of `targets` on one device may be relied on, other than what follows from the above.
Results may differ from a plain program's by a relative error of at most 0.0065.
Values may be sent and summed in bfloat16 or wider, within the bound.
A program may use at most 320 MiB of HBM per device.

v0:
```python
import jax
import jax.numpy as jnp
from jax import lax
from jax.sharding import PartitionSpec as P

loss_scale = 0.25
tile_rows = 64


def arrange(arrived_ids, block_count, buffer_rows):
    block_hot = (arrived_ids[:, None] == jnp.arange(block_count, dtype=jnp.int32)[None, :]).astype(
        jnp.int32
    )
    counts = jnp.sum(block_hot, axis=0)
    rank = jnp.sum((jnp.cumsum(block_hot, axis=0) - block_hot) * block_hot, axis=1)
    padded_counts = (counts + tile_rows - 1) // tile_rows * tile_rows
    offsets = jnp.cumsum(padded_counts) - padded_counts
    ends = offsets + padded_counts
    padded_row_total = ((buffer_rows + tile_rows - 1) // tile_rows + block_count) * tile_rows
    tile_count = padded_row_total // tile_rows
    valid = arrived_ids >= 0
    position = jnp.where(
        valid, jnp.sum(block_hot * offsets[None, :], axis=1) + rank, padded_row_total
    )
    tile_start = jnp.arange(tile_count, dtype=jnp.int32) * tile_rows
    tile_block = jnp.minimum(
        jnp.sum((ends[None, :] <= tile_start[:, None]).astype(jnp.int32), axis=1), block_count - 1
    )
    reading = jnp.minimum(position, padded_row_total - 1)
    return (position, reading, tile_block, padded_row_total)


def to_tiles(rows, position, padded_row_total):
    width = rows.shape[1]
    filled = jnp.zeros((padded_row_total, width), rows.dtype).at[position].set(rows, mode="drop")
    return filled.reshape(padded_row_total // tile_rows, tile_rows, width)


def shards(queries_in, classifier, owner_ids, local_ids, targets):
    groups = lax.axis_size("labels")
    query_row_block, feature_width = queries_in.shape
    shortlist = owner_ids.shape[1]
    block_width = targets.shape[2]
    label_rows = classifier.shape[0]
    block_count = label_rows // block_width
    capacity = min(query_row_block, query_row_block * 16 // groups)
    buffer_rows = groups * capacity
    weight_blocks = classifier.reshape(block_count, block_width, feature_width)
    flat_owner = owner_ids.reshape(-1)
    flat_local = local_ids.reshape(-1)
    onehot = (flat_owner[:, None] == jnp.arange(groups, dtype=jnp.int32)[None, :]).astype(jnp.int32)
    before = jnp.cumsum(onehot, axis=0) - onehot
    slot_rank = jnp.sum(before * onehot, axis=1)
    slot_index = flat_owner * capacity + slot_rank
    repeated = jnp.repeat(queries_in, shortlist, axis=0)
    sent_ids = jnp.full((buffer_rows,), -1, jnp.int32).at[slot_index].set(flat_local)
    sent_rows = jnp.zeros((buffer_rows, feature_width), jnp.bfloat16).at[slot_index].set(repeated)
    arrived, arrived_ids = (
        lax.all_to_all(
            sent_rows.reshape(groups, capacity, feature_width),
            "labels",
            split_axis=0,
            concat_axis=0,
            tiled=True,
        ),
        lax.all_to_all(
            sent_ids.reshape(groups, capacity), "labels", split_axis=0, concat_axis=0, tiled=True
        ),
    )
    arrived = arrived.reshape(buffer_rows, feature_width)
    arrived_ids = arrived_ids.reshape(buffer_rows)
    position, reading, tile_block, padded_row_total = arrange(arrived_ids, block_count, buffer_rows)
    tile_weights = weight_blocks[tile_block]
    tile_feats = to_tiles(arrived, position, padded_row_total)
    tile_logits = jnp.einsum(
        "trd,tkd->trk", tile_feats, tile_weights, preferred_element_type=jnp.float32
    ).astype(jnp.bfloat16)
    picked = tile_logits.reshape(padded_row_total, block_width)[reading]
    returned = lax.all_to_all(
        picked.reshape(groups, capacity, block_width),
        "labels",
        split_axis=0,
        concat_axis=0,
        tiled=True,
    )
    logits = (
        returned.reshape(buffer_rows, block_width)[slot_index]
        .reshape(query_row_block, shortlist, block_width)
        .astype(jnp.float32)
    )
    label_float = targets.astype(jnp.float32)
    query_loss = jnp.sum(jax.nn.softplus(logits) - label_float * logits, axis=(1, 2)) * loss_scale
    loss_grads = ((jax.nn.sigmoid(logits) - label_float) * loss_scale).astype(jnp.bfloat16)
    grad_buffer = (
        jnp.zeros((buffer_rows, block_width), jnp.bfloat16)
        .at[slot_index]
        .set(loss_grads.reshape(-1, block_width))
    )
    grad_rows = lax.all_to_all(
        grad_buffer.reshape(groups, capacity, block_width),
        "labels",
        split_axis=0,
        concat_axis=0,
        tiled=True,
    ).reshape(buffer_rows, block_width)
    grad_tiles = to_tiles(grad_rows, position, padded_row_total)
    tile_terms = jnp.einsum(
        "trk,tkd->trd", grad_tiles, tile_weights, preferred_element_type=jnp.float32
    ).astype(jnp.bfloat16)
    feature_terms = tile_terms.reshape(padded_row_total, feature_width)[reading]
    tile_partial_sum = jnp.einsum(
        "trk,trd->tkd", grad_tiles, tile_feats, preferred_element_type=jnp.float32
    )
    tile_onehot_mask = (
        tile_block[:, None] == jnp.arange(block_count, dtype=jnp.int32)[None, :]
    ).astype(jnp.float32)
    partial_grad = jnp.einsum(
        "vi,vyf->iyf", tile_onehot_mask, tile_partial_sum, precision=lax.Precision.HIGHEST
    )
    weight_grad = lax.psum_scatter(
        partial_grad.reshape(label_rows, feature_width), "queries", scatter_dimension=0, tiled=True
    ).astype(jnp.bfloat16)
    returned_grads = lax.all_to_all(
        feature_terms.reshape(groups, capacity, feature_width),
        "labels",
        split_axis=0,
        concat_axis=0,
        tiled=True,
    ).reshape(buffer_rows, feature_width)
    feature_grad = jnp.sum(
        returned_grads[slot_index]
        .reshape(query_row_block, shortlist, feature_width)
        .astype(jnp.float32),
        axis=1,
    )
    return (query_loss, feature_grad, weight_grad)


def solution(mesh):
    in_specs = (
        P(("queries", "labels"), None),
        P("labels", None),
        P(("queries", "labels"), None),
        P(("queries", "labels"), None),
        P(("queries", "labels"), None, None),
    )
    out_specs = (
        P(("queries", "labels")),
        P(("queries", "labels"), None),
        P(("labels", "queries"), None),
    )
    return jax.shard_map(shards, mesh=mesh, in_specs=in_specs, out_specs=out_specs, check_vma=False)
```

profile of v0, /device:TPU:0, one launch (start us, length us, event | category | flops | bytes accessed | tf_op | source)
XLA Modules:
  0.0 473.9 jit_solution(14438463321522025654)
XLA Ops:
  7.2 0.9 broadcast_multiply_fusion
  8.0 0.9 copy.27
  9.2 0.1 copy.26
  9.3 0.1 mul.73
  9.4 0.8 copy.31
  10.4 0.7 fusion.31
  11.1 15.9 %reduce-window.20 = s32[32,16,128]{2,1,0:T(8,128)S(1)} reduce-window(s32[32,16,128]{2,1,0:T(8,128)} %fusion.31, s32[]{:T(128)} %constant.24.clone.1), window={size=1x1x128 pad=0_0x0_0x127_0}, to_apply=%region_0.0 | reduce-window | flops 8323072 | bytes 524292 | tf_op jit(solution)/shard_map/reduce-window
  27.0 0.8 slice.26
  27.8 1.2 copy.35
  29.0 0.2 reduce-window.21
  29.2 0.1 broadcast_add_fusion.1
  29.5 8.6 %scatter_custom_fusion = s32[4096]{0:T(1024)} fusion(s32[2048]{0:T(1024)S(1)} %bitcast.125, s32[2048]{0:T(1024)S(1)} %reshape.379, s32[]{:T(128)} %constant.22.clone.1), kind=kCustom, calls=%fused_computation.69 | custom fusion | bytes 16388 | tf_op jit(solution)/shard_map/scatter | solution.py:56
  38.1 8.4 %all-to-all-start = ((s32[32,1,128]{2,1,0:T(1,128)}), s32[32,1,128]{2,1,0:T(1,128)S(1)}, u32[]{:S(2)}, u32[]{:S(2)}) async-start(s32[32,1,128]{2,1,0:T(1,128)} %bitcast.5), calls=%async_computation | async-start | bytes 32768 | tf_op jit(solution)/shard_map/all_to_all | solution.py:66
  46.5 13.8 %scatter_custom_fusion.1 = bf16[4096,768]{1,0:T(8,128)(2,1)} fusion(s32[2048]{0:T(1024)S(1)} %bitcast.126, bf16[]{:T(256)} %constant.21.clone.1, bf16[256,768]{1,0:T(8,128)(2,1)} %param.5), kind=kCustom, calls=%fused_computation.16 | custom fusion | bytes 6684674 | tf_op jit(solution)/shard_map/scatter | solution.py:57
  60.3 7.7 %all-to-all-start.1 = ((bf16[32,128,768]{2,1,0:T(8,128)(2,1)}), bf16[32,128,768]{2,1,0:T(8,128)(2,1)}, u32[]{:S(2)}, u32[]{:S(2)}) async-start(bf16[32,128,768]{2,1,0:T(8,128)(2,1)} %bitcast.110), calls=%async_computation.1 | async-start | bytes 12582912 | tf_op jit(solution)/shard_map/all_to_all | solution.py:59
  68.0 0.1 convert_reduce_fusion.1
  68.3 0.1 reduce
  68.4 0.7 fusion.32
  69.1 8.3 %reduce-window.30 = s32[16,32,128]{2,1,0:T(8,128)S(1)} reduce-window(s32[16,32,128]{2,1,0:T(8,128)} %fusion.32, s32[]{:T(128)} %constant.24.clone.1), window={size=1x1x128 pad=0_0x0_0x127_0}, to_apply=%region_7.8 | reduce-window | flops 8323072 | bytes 524292 | tf_op jit(solution)/shard_map/reduce-window.3
  77.4 0.5 slice_reduce_fusion
  77.9 0.2 reduce-window.31
  78.1 0.1 broadcast_add_fusion
  78.2 0.2 fusion.27
  78.6 8.1 %gather_fusion = bf16[80,128,768]{2,1,0:T(8,128)(2,1)} fusion(bf16[16,128,768]{2,1,0:T(8,128)(2,1)S(1)} %bitcast.102, s32[1024]{0:T(1024)S(1)} %pad_clamp_fusion), kind=kCustom, calls=%fused_computation | custom fusion | bytes 31457600 | tf_op jit(solution)/shard_map/gather | solution.py:73
  86.8 59.0 %all-to-all-done.1 = bf16[32,128,768]{2,1,0:T(8,128)(2,1)} async-done(((bf16[32,128,768]{2,1,0:T(8,128)(2,1)}), bf16[32,128,768]{2,1,0:T(8,128)(2,1)}, u32[]{:S(2)}, u32[]{:S(2)}) %all-to-all-start.1) | async-done | bytes 6291488 | tf_op jit(solution)/shard_map/all_to_all | solution.py:59
  145.8 23.6 %scatter_custom_fusion.2 = bf16[5120,768]{1,0:T(8,128)(2,1)} fusion(s32[4096]{0:T(1024)S(1)} %bitcast.129, bf16[4096,768]{1,0:T(8,128)(2,1)} %bitcast.15, bf16[]{:T(256)} %constant.21.clone.1), kind=kCustom, calls=%fused_computation.14 | custom fusion | bytes 7864832 | tf_op jit(solution)/shard_map/scatter | solution.py:35
  169.5 11.8 %convolution_convert_fusion.1 = bf16[80,64,128]{2,1,0:T(8,128)(2,1)S(1)} fusion(bf16[80,64,768]{2,1,0:T(8,128)(2,1)} %bitcast.104, bf16[80,128,768]{2,1,0:T(8,128)(2,1)} %gather_fusion), kind=kOutput, calls=%fused_computation.24 | convolution fusion | flops 1007288320 | bytes 24903680 | tf_op jit(solution)/shard_map/trd,tkd->trk/dot_general | solution.py:75
  181.3 14.9 %gather_fusion.1 = bf16[4096,128]{1,0:T(8,128)(2,1)} fusion(bf16[5120,128]{1,0:T(8,128)(2,1)S(1)} %bitcast.106, s32[4096]{0:T(1024)S(1)} %broadcast_clamp_fusion), kind=kCustom, calls=%fused_computation.1 | custom fusion | bytes 2113536 | tf_op jit(solution)/shard_map/gather | solution.py:78
  196.2 4.1 all-to-all-start.2
  200.3 17.3 %all-to-all-done.2 = bf16[32,128,128]{2,1,0:T(8,128)(2,1)S(1)} async-done(((bf16[32,128,128]{2,1,0:T(8,128)(2,1)}), bf16[32,128,128]{2,1,0:T(8,128)(2,1)S(1)}, u32[]{:S(2)}, u32[]{:S(2)}) %all-to-all-start.2) | async-done | bytes 1048608 | tf_op jit(solution)/shard_map/all_to_all | solution.py:79
  217.6 6.2 %gather_fusion.2 = bf16[2048,128]{1,0:T(8,128)(2,1)S(1)} fusion(bf16[4096,128]{1,0:T(8,128)(2,1)S(1)} %bitcast.109, s32[2048]{0:T(1024)S(1)} %broadcast_clamp_fusion.1), kind=kCustom, calls=%fused_computation.2 | custom fusion | bytes 1056768 | tf_op jit(solution)/shard_map/gather | solution.py:87
  223.8 7.1 %scatter_custom_fusion.3 = bf16[4096,128]{1,0:T(8,128)(2,1)} fusion(s32[2048]{0:T(1024)S(1)} %bitcast.128, bf16[]{:T(256)} %constant.21.clone.1, s32[256,8,128]{2,1,0:T(8,128)S(1)} %copy-done.2, bf16[2048,128]{1,0:T(8,128)(2,1)S(1)} %gather_fusion.2, f32[]{:T(128)} %constant.65.clone.1, f32[]{:T(128)} %constant.66.clone.1), kind=kCustom, calls=%fused_computation.40 | custom fusion | flops 2097152 | bytes 2621450 | tf_op jit(solution)/shard_map/scatter | solution.py:97
  230.9 3.9 all-to-all-start.3
  234.9 17.3 %all-to-all-done.3 = bf16[32,128,128]{2,1,0:T(8,128)(2,1)S(1)} async-done(((bf16[32,128,128]{2,1,0:T(8,128)(2,1)}), bf16[32,128,128]{2,1,0:T(8,128)(2,1)S(1)}, u32[]{:S(2)}, u32[]{:S(2)}) %all-to-all-start.3) | async-done | bytes 1048608 | tf_op jit(solution)/shard_map/all_to_all | solution.py:99
  252.2 1.0 copy-done.3
  253.2 11.6 %scatter_custom_fusion.4 = bf16[5120,128]{1,0:T(8,128)(2,1)S(1)} fusion(s32[4096]{0:T(1024)S(1)} %bitcast.130, bf16[4096,128]{1,0:T(8,128)(2,1)} %bitcast.113, bf16[]{:T(256)} %constant.21.clone.1), kind=kCustom, calls=%fused_computation.38 | custom fusion | bytes 1311232 | tf_op jit(solution)/shard_map/scatter | solution.py:35
  264.8 17.9 %fusion.40 = f32[80,128,768]{2,1,0:T(8,128)} fusion(bf16[80,64,128]{2,1,0:T(8,128)(2,1)S(1)} %bitcast.107, bf16[80,64,768]{2,1,0:T(8,128)(2,1)} %bitcast.105), kind=kOutput, calls=%fused_computation.92 | convolution fusion | flops 1006632960 | bytes 40632320 | tf_op jit(solution)/shard_map/trk,trd->tkd/dot_general | solution.py:111
  282.6 37.0 %fusion = f32[16,128,768]{2,0,1:T(8,128)} fusion(f32[80,128,768]{2,1,0:T(8,128)} %fusion.40, s32[80]{0:T(128)S(1)} %broadcast_minimum_fusion), kind=kOutput, calls=%fused_computation.10 | convolution fusion | flops 1509950720 | bytes 37749056 | tf_op jit(solution)/shard_map/vi,vyf->iyf/dot_general | solution.py:117
  319.6 9.1 %copy.34 = f32[16,128,768]{2,1,0:T(8,128)} copy(f32[16,128,768]{2,0,1:T(8,128)} %fusion) | data formatting | bytes 12582912 | tf_op jit(solution)/shard_map/vi,vyf->iyf/dot_general | solution.py:117
  328.8 10.8 %convolution_convert_fusion = bf16[80,64,768]{2,1,0:T(8,128)(2,1)} fusion(bf16[80,64,128]{2,1,0:T(8,128)(2,1)S(1)} %bitcast.108, bf16[80,128,768]{2,1,0:T(8,128)(2,1)} %gather_fusion), kind=kOutput, calls=%fused_computation.12 | convolution fusion | flops 1010565120 | bytes 24903680 | tf_op jit(solution)/shard_map/trk,tkd->trd/dot_general | solution.py:107
  339.6 23.3 %gather_fusion.3 = bf16[4096,768]{1,0:T(8,128)(2,1)} fusion(bf16[5120,768]{1,0:T(8,128)(2,1)} %bitcast.103, s32[4096]{0:T(1024)S(1)} %broadcast_clamp_fusion), kind=kCustom, calls=%fused_computation.3 | custom fusion | bytes 12599296 | tf_op jit(solution)/shard_map/gather | solution.py:110
  362.9 5.1 %all-to-all-start.4 = ((bf16[32,128,768]{2,1,0:T(8,128)(2,1)}), bf16[32,128,768]{2,1,0:T(8,128)(2,1)}, u32[]{:S(2)}, u32[]{:S(2)}) async-start(bf16[32,128,768]{2,1,0:T(8,128)(2,1)} %bitcast.112), calls=%async_computation.4 | async-start | bytes 12582912 | tf_op jit(solution)/shard_map/all_to_all | solution.py:123
  368.0 1.3 fusion.18
  369.3 0.6 broadcast_multiply_fusion.1
  369.9 75.9 %all-to-all-done.4 = bf16[32,128,768]{2,1,0:T(8,128)(2,1)} async-done(((bf16[32,128,768]{2,1,0:T(8,128)(2,1)}), bf16[32,128,768]{2,1,0:T(8,128)(2,1)}, u32[]{:S(2)}, u32[]{:S(2)}) %all-to-all-start.4) | async-done | bytes 6291488 | tf_op jit(solution)/shard_map/all_to_all | solution.py:123
  445.8 13.8 %gather_fusion.4 = bf16[2048,768]{1,0:T(8,128)(2,1)} fusion(bf16[4096,768]{1,0:T(8,128)(2,1)} %bitcast.32, s32[2048]{0:T(1024)S(1)} %broadcast_clamp_fusion.1), kind=kCustom, calls=%fused_computation.4 | custom fusion | bytes 6299648 | tf_op jit(solution)/shard_map/gather | solution.py:131
  459.6 4.8 %convert_reduce_fusion = f32[256,768]{1,0:T(8,128)} fusion(bf16[2048,768]{1,0:T(8,128)(2,1)} %gather_fusion.4), kind=kLoop, calls=%fused_computation.13 | loop fusion | flops 2949120 | bytes 3932160 | tf_op jit(solution)/shard_map/reduce_sum | solution.py:130
  464.4 2.4 convert_element_type.58
  (29 shorter events, 0.9 us)
Async XLA Ops:
  7.2 71.5 %copy-start = (bf16[2048,768]{1,0:T(8,128)(2,1)S(1)}, bf16[2048,768]{1,0:T(8,128)(2,1)}, u32[]{:S(2)}) copy-start(bf16[2048,768]{1,0:T(8,128)(2,1)} %param.6) | copy-start | bytes 9437188
  38.1 22.2 %all-to-all-start = ((s32[32,1,128]{2,1,0:T(1,128)}), s32[32,1,128]{2,1,0:T(1,128)S(1)}, u32[]{:S(2)}, u32[]{:S(2)}) async-start(s32[32,1,128]{2,1,0:T(1,128)} %bitcast.5), calls=%async_computation | async-start | bytes 32768 | tf_op jit(solution)/shard_map/all_to_all | solution.py:66
  60.3 85.5 %all-to-all-start.1 = ((bf16[32,128,768]{2,1,0:T(8,128)(2,1)}), bf16[32,128,768]{2,1,0:T(8,128)(2,1)}, u32[]{:S(2)}, u32[]{:S(2)}) async-start(bf16[32,128,768]{2,1,0:T(8,128)(2,1)} %bitcast.110), calls=%async_computation.1 | async-start | bytes 12582912 | tf_op jit(solution)/shard_map/all_to_all | solution.py:59
  181.3 42.6 %copy-start.2 = (s32[256,8,128]{2,1,0:T(8,128)S(1)}, s32[256,8,128]{2,1,0:T(8,128)}, u32[]{:S(2)}) copy-start(s32[256,8,128]{2,1,0:T(8,128)} %param.9) | copy-start | bytes 3145732
  196.2 21.5 %all-to-all-start.2 = ((bf16[32,128,128]{2,1,0:T(8,128)(2,1)}), bf16[32,128,128]{2,1,0:T(8,128)(2,1)S(1)}, u32[]{:S(2)}, u32[]{:S(2)}) async-start(bf16[32,128,128]{2,1,0:T(8,128)(2,1)} %bitcast.22), calls=%async_computation.2 | async-start | bytes 2097152 | tf_op jit(solution)/shard_map/all_to_all | solution.py:79
  230.9 21.3 %all-to-all-start.3 = ((bf16[32,128,128]{2,1,0:T(8,128)(2,1)}), bf16[32,128,128]{2,1,0:T(8,128)(2,1)S(1)}, u32[]{:S(2)}, u32[]{:S(2)}) async-start(bf16[32,128,128]{2,1,0:T(8,128)(2,1)} %bitcast.27), calls=%async_computation.3 | async-start | bytes 2097152 | tf_op jit(solution)/shard_map/all_to_all | solution.py:99
  234.9 229.6 %reduce-scatter.2.cloned.1.call-start = ((), (), s32[]{:S(2)}) async-start(), calls=%async_computation.6 | async-start | bytes 7864320 | tf_op jit(solution)/shard_map/reduce_scatter | solution.py:120
  252.2 1.0 copy-start.3
  362.9 82.9 %all-to-all-start.4 = ((bf16[32,128,768]{2,1,0:T(8,128)(2,1)}), bf16[32,128,768]{2,1,0:T(8,128)(2,1)}, u32[]{:S(2)}, u32[]{:S(2)}) async-start(bf16[32,128,768]{2,1,0:T(8,128)(2,1)} %bitcast.112), calls=%async_computation.4 | async-start | bytes 12582912 | tf_op jit(solution)/shard_map/all_to_all | solution.py:123
  445.8 21.0 %copy-start.1 = (bf16[2048,768]{1,0:T(8,128)(2,1)S(1)}, bf16[2048,768]{1,0:T(8,128)(2,1)}, u32[]{:S(2)}) copy-start(bf16[2048,768]{1,0:T(8,128)(2,1)} %param.6) | copy-start | bytes 9437188
Sparse Core Ops, SparseCore 0:
  328.9 61.5 reduce-scatter.1
where the time goes:
time: 482 us; the launch traced here: 474 us
  waiting for transfers between devices  169 us (35%)
  local copies, waits for them, and re-layouts  139 us (29%)
  matrix products  77.5 us (16%)
  other arithmetic  44.2 us (9%)
  starting transfers between devices  29.3 us (6%)
  between operations  14.5 us (3%)
    all_to_all x1, waiting for transfers between devices, shards(): lax.all_to_all(feature_terms.reshape(groups, capacity, feature_width), 'l...  75.9 us
    all_to_all x1, waiting for transfers between devices, shards(): lax.all_to_all(sent_rows.reshape(groups, capacity, feature_width), 'label...  59 us
    dot_general x1, matrix products, shards(): jnp.einsum('vi,vyf->iyf', tile_onehot_mask, tile_partial_sum, precision=l...  37 us
    scatter x2, local copies, waits for them, and re-layouts, to_tiles(): jnp.zeros((padded_row_total, width), rows.dtype).at[position]  35.2 us
    another operation x8, other arithmetic  25 us
    gather x1, local copies, waits for them, and re-layouts, shards(): feature_terms = tile_terms.reshape(padded_row_total, feature_width)[reading]  23.3 us
    dot_general x1, matrix products, shards(): jnp.einsum('trk,trd->tkd', grad_tiles, tile_feats, preferred_element_type...  17.9 us
    all_to_all x1, waiting for transfers between devices, shards(): lax.all_to_all(picked.reshape(groups, capacity, block_width), 'labels', s...  17.3 us
  transfers between devices with their start and end apart: 6, of which 4 were waited for; matrix products, arithmetic and copies ran while one was open for 18% of the time, Pallas kernels for 0%

commit v1 on v0

v1 whole, which is shorter than its diff:
```python
import jax
import jax.numpy as jnp
from jax import lax
from jax.experimental import pallas as pl
from jax.experimental.pallas import tpu as pltpu
from jax.sharding import PartitionSpec as P

MESH = pl.DeviceIdType.MESH
BF = jnp.bfloat16
F32 = jnp.float32

ORDER = [
    (0, 0), (0, 1), (1, 0), (0, 3), (3, 0), (0, 2), (2, 0), (1, 1),
    (1, 3), (3, 1), (1, 2), (2, 1), (3, 3), (3, 2), (2, 3), (2, 2),
]
SLOT = {chip: k for k, chip in enumerate(ORDER)}
MIRROR = [SLOT[(b, a)] for a, b in ORDER]
PAY = 144


def slot(a, b):
    return SLOT[(a % 4, b % 4)]


def nt(a, b):
    return lax.dot_general(a, b, (((1,), (1,)), ((), ())), preferred_element_type=F32)


def nn(a, b):
    return jnp.dot(a, b, preferred_element_type=F32)


def one_chunk(k, own, sib, pay, w, wt, rows, grads, terms0, terms1, loss_out):
    half = lax.rem(k, 2)
    spot = lax.broadcasted_iota(jnp.int32, (128, 128), 0).astype(F32) + 1.0
    picks, ids = [], []
    for core, src in enumerate((own, sib)):
        tail = pay[core, k, 128:144, :].astype(F32)
        ids.append(tail[0:1, :])
        pick = jnp.concatenate(
            [jnp.where(spot == tail[r : r + 1, :], 1.0, 0.0) for r in (1, 2)], axis=1
        )
        picks.append(pick)
        rows[half, core * 128 : core * 128 + 128, :] = nn(pick.astype(BF), src[k]).astype(BF)
    ids = jnp.concatenate(ids, axis=1)
    x = rows[half]
    z = jnp.zeros((128, 256), F32)
    for part in range(2):
        scores = nt(w[part * 1024 : part * 1024 + 1024, :], x)
        for b in range(8):
            z = jnp.where(ids == float(part * 8 + b + 1), scores[b * 128 : b * 128 + 128, :], z)
    z = z.astype(BF).astype(F32)
    y = jnp.concatenate([pay[core, k, 0:128, :] for core in (0, 1)], axis=1).astype(F32)
    valid = jnp.where(ids > 0.5, 0.25, 0.0)
    e = jnp.exp(-jnp.abs(z))
    loss = jnp.sum(jnp.maximum(z, 0.0) + jnp.log1p(e) - y * z, axis=0, keepdims=True) * valid
    sig = jnp.where(z >= 0.0, 1.0, e) / (1.0 + e)
    g = (sig - y) * valid
    for b in range(16):
        grads[half, b * 128 : b * 128 + 128, :] = jnp.where(ids == float(b + 1), g, 0.0).astype(BF)
    ft = nn(wt[...], grads[half]).astype(BF)
    place = lax.broadcasted_iota(jnp.int32, (16, 128), 0)
    for core, terms in enumerate((terms0, terms1)):
        index = k if core == 0 else lax.rem(k, 4)
        pick = picks[core]
        terms[index] = nt(pick.T.astype(BF), ft[:, core * 128 : core * 128 + 128]).astype(BF)
        part = loss[:, core * 128 : core * 128 + 128]
        high = part.astype(BF).astype(F32)
        mid = (part - high).astype(BF).astype(F32)
        low = part - high - mid
        stack = jnp.where(place == 0, high, jnp.where(place == 1, mid, jnp.where(place == 2, low, 0.0)))
        spread = nn(stack.astype(BF), pick.astype(BF))
        loss_out[core, k] = jnp.broadcast_to(jnp.sum(spread, axis=0, keepdims=True), (8, 256))


def add_weight(rows, grads, total):
    def step(m, _):
        at = pl.ds(pl.multiple_of(m * 512, 512), 512)
        total[at, :] += nn(grads[0, at, :], rows[0]) + nn(grads[1, at, :], rows[1])
        return 0

    lax.fori_loop(0, 4, step, 0)


def kernel(
    q_ref, w, wt, labels_in, owner_ref, rank_ref, tail_ref,
    loss_ref, feat_ref, weight_ref,
    own, sib, pay_out, pay, terms0, terms1, back, half_in, full_in, half_a, full_a,
    total, half_x, full_x, rows, grads, loss_out, loss_in,
    own_s, own_r, sib_s, sib_r, pay_s, pay_r, back_s, back_r, rs_s, rs_r, loss_s, loss_r,
):
    me = lax.axis_index("labels")
    mx = lax.axis_index("queries")
    core = lax.rem(me, 2)
    my = lax.rem(me // 2, 4)
    mz = me // 8

    def dev(a, b, c=0):
        dz = a * (1 - core) + b * core
        dy = b * (1 - core) + a * core
        return (lax.rem(mz + dz, 4) * 4 + lax.rem(my + dy, 4)) * 2 + lax.rem(core + c, 2)

    def to(device, src, dst, ssem, rsem):
        return pltpu.make_async_remote_copy(
            src_ref=src, dst_ref=dst, send_sem=ssem, recv_sem=rsem,
            device_id={"labels": device}, device_id_type=MESH,
        )

    def to_x(step, src, dst, ssem, rsem):
        return pltpu.make_async_remote_copy(
            src_ref=src, dst_ref=dst, send_sem=ssem, recv_sem=rsem,
            device_id={"queries": lax.rem(mx + step, 4)}, device_id_type=MESH,
        )

    barrier = pltpu.get_barrier_semaphore()

    def greet(i, _):
        pl.semaphore_signal(
            barrier, inc=1, device_id={"labels": lax.rem(me + i, 32)}, device_id_type=MESH
        )
        return 0

    lax.fori_loop(1, 32, greet, 0)
    for step in (1, 3):
        pl.semaphore_signal(
            barrier, inc=1, device_id={"queries": lax.rem(mx + step, 4)}, device_id_type=MESH
        )
    pl.semaphore_wait(barrier, 33)

    sent = []

    def go(make):
        make().start()
        sent.append(make)

    def rows_of(ref, half):
        return ref if half is None else ref.at[pl.ds(half * 128, 128), :]

    def pass_on(k):
        a, b = ORDER[k]
        sends = []
        if b == 0:
            if a == 0:
                sends += [(1, 0, None), (3, 0, None)]
            if a == 3:
                sends.append((1, 0, 0))
            if a == 1:
                sends.append((3, 0, 1))
            sends += [(0, 1, None), (0, 3, None)]
        if b == 3:
            sends.append((0, 1, 0))
        if b == 1:
            sends.append((0, 3, 1))
        for n, (sa, sb, half) in enumerate(sends):
            there = slot(a - sa, b - sb)
            go(
                lambda sa=sa, sb=sb, half=half, there=there, n=n: to(
                    dev(sa, sb),
                    rows_of(own.at[k], half),
                    rows_of(own.at[there], half),
                    own_s.at[k * 4 + n],
                    own_r.at[there * 2 + (half or 0)],
                )
            )
        go(lambda: to(dev(0, 0, 1), own.at[k], sib.at[MIRROR[k]], sib_s.at[k], sib_r.at[MIRROR[k]]))

    def arrive(k):
        a, b = ORDER[k]
        halves = (0, 1) if b == 2 or (b == 0 and a == 2) else (None,)
        for half in halves:
            ref = rows_of(own.at[k], half)
            to(dev(0, 0, 1), ref, ref, own_s.at[k * 4], own_r.at[k * 2 + (half or 0)]).wait_recv()
        pass_on(k)

    own[0] = q_ref[...]
    pass_on(0)

    spot = lax.broadcasted_iota(jnp.int32, (128, 2048), 0)
    first = lax.broadcasted_iota(jnp.int32, (16, 128), 0) == 0

    def pack(group, _):
        owners = owner_ref[...]
        ranks = rank_ref[...]
        stack = jnp.concatenate(
            [
                jnp.where(spot == jnp.where(owners == group * 4 + i, ranks, -1), 1.0, 0.0).astype(BF)
                for i in range(4)
            ],
            axis=0,
        )
        found = nn(stack, labels_in[...])
        for i in range(4):
            piece = found[i * 128 : i * 128 + 128, :]
            o = group * 4 + i
            pay_out[o, 0:128, :] = piece[:, 0:128].T.astype(BF)
            ids = piece[:, 128:256].T[0:16, :]
            pay_out[o, 128:144, :] = (jnp.where(first, ids, 0.0) + tail_ref[o]).astype(BF)
        return 0

    lax.fori_loop(0, 8, pack, 0)
    pay[0, 0] = pay_out[me]
    for k, (a, b) in enumerate(ORDER):
        for c in (0, 1):
            if k == 0 and c == 0:
                continue
            there = slot(-a, -b) if c == 0 else slot(-b, -a)

            def make(a=a, b=b, c=c, k=k, there=there):
                d = dev(a, b, c)
                return to(d, pay_out.at[d], pay.at[c, there], pay_s.at[c * 16 + k], pay_r.at[c * 16 + there])

            go(make)

    def halves_of(buf, index, a_axis, store, sem):
        for h in (0, 1):
            step = 1 if h == 0 else 3
            d = (step, 0) if a_axis else (0, step)
            go(
                lambda d=d, h=h: to(
                    dev(*d), rows_of(buf.at[index], h), store(h), rs_s.at[sem + h], rs_r.at[sem + h]
                )
            )

    def fulls_of(buf, plus, minus, a_axis, store, sem):
        for h, index in enumerate((plus, minus)):
            step = 1 if h == 0 else 3
            d = (step, 0) if a_axis else (0, step)
            go(
                lambda d=d, h=h, index=index: to(
                    dev(*d), buf.at[index], store(h), rs_s.at[sem + 2 + h], rs_r.at[sem + 2 + h]
                )
            )

    def got(store, h, sem):
        to(dev(0, 0, 1), store(h), store(h), rs_s.at[sem], rs_r.at[sem]).wait_recv()

    def stage1(a):
        for b in (2, 1, 3, 0):
            k = slot(a, b)
            far = MIRROR[k]
            to(dev(0, 0, 1), back.at[far], back.at[far], back_s.at[far], back_r.at[far]).wait_recv()
            terms0[k] = terms0[k] + back[far]
            if b == 2:
                halves_of(terms0, k, False, lambda h: half_in.at[a, h], a * 4)

    def meet(buf, plus, minus, store, sem):
        got(store, 0, sem)
        buf[plus, 0:128, :] = buf[plus, 0:128, :] + store(0)[...]
        got(store, 1, sem + 1)
        buf[minus, 128:256, :] = buf[minus, 128:256, :] + store(1)[...]

    def stage2(a):
        plus, minus = slot(a, 1), slot(a, 3)
        meet(terms0, plus, minus, lambda h: half_in.at[a, h], a * 4)
        fulls_of(terms0, plus, minus, False, lambda h: full_in.at[a, h], a * 4)

    def stage3(a):
        for h in (0, 1):
            got(lambda h: full_in.at[a, h], h, a * 4 + 2 + h)
        k = slot(a, 0)
        terms0[k] = (
            terms0[k].astype(F32) + full_in[a, 0].astype(F32) + full_in[a, 1].astype(F32)
        ).astype(BF)

    acts = {
        1: [lambda: [arrive(k) for k in (1, 2, 3, 4)]],
        3: [lambda: [arrive(k) for k in (5, 6)]],
        4: [lambda: [arrive(k) for k in (7, 8, 9, 12)]],
        6: [lambda: [arrive(k) for k in (10, 11, 13, 14)]],
        8: [lambda: stage1(0)],
        9: [lambda: arrive(15)],
        10: [lambda: stage2(0)],
        12: [lambda: stage3(0)],
        13: [lambda: stage1(1)],
        14: [lambda: stage2(1)],
        15: [lambda: stage3(1), lambda: stage1(3)],
    }

    def send_back(k, index):
        return to(dev(0, 0, 1), terms1.at[index], back.at[k], back_s.at[k], back_r.at[k])

    total[...] = jnp.zeros_like(total)

    def step(k, _):
        for when, todo in acts.items():

            @pl.when(k == when)
            def _():
                for act in todo:
                    act()

        to(dev(0, 0, 1), sib.at[k], sib.at[k], sib_s.at[k], sib_r.at[k]).wait_recv()

        @pl.when(k > 0)
        def _():
            to(dev(0, 0, 1), pay.at[0, k], pay.at[0, k], pay_s.at[k], pay_r.at[k]).wait_recv()

        to(dev(0, 0, 1), pay.at[1, k], pay.at[1, k], pay_s.at[16 + k], pay_r.at[16 + k]).wait_recv()

        @pl.when(k >= 4)
        def _():
            send_back(k - 4, lax.rem(k, 4)).wait_send()

        one_chunk(k, own, sib, pay, w, wt, rows, grads, terms0, terms1, loss_out)
        send_back(k, lax.rem(k, 4)).start()

        @pl.when(lax.rem(k, 2) == 1)
        def _():
            add_weight(rows, grads, total)

        return 0

    lax.fori_loop(0, 16, step, 0)
    for k in range(12, 16):
        send_back(k, k % 4).wait_send()

    def shard(dx):
        return pl.ds(pl.multiple_of(lax.rem(mx + dx, 4) * 512, 512), 512)

    for dx in (2, 1, 3):
        block = total[shard(dx), :].astype(BF)
        for h in (0, 1):
            sib[(dx - 1) * 2 + h] = block[h * 256 : h * 256 + 256, :]
        if dx == 2:
            for h in (0, 1):
                go(
                    lambda h=h: to_x(
                        1 if h == 0 else 3, sib.at[2 + h], half_x.at[h], rs_s.at[20 + h], rs_r.at[20 + h]
                    )
                )
    stage1(2)

    for k, (a, b) in enumerate(ORDER):
        for c in (0, 1):
            if k == 0 and c == 0:
                continue
            there = slot(-a, -b) if c == 0 else slot(-b, -a)
            go(
                lambda a=a, b=b, c=c, k=k, there=there: to(
                    dev(a, b, c), loss_out.at[c, k], loss_in.at[c, there],
                    loss_s.at[c * 16 + k], loss_r.at[c * 16 + there],
                )
            )
    stage2(3)
    for h in (0, 1):
        to_x(1, half_x.at[h], half_x.at[h], rs_s.at[20 + h], rs_r.at[20 + h]).wait_recv()
    sib[0] = sib[0] + half_x[0]
    sib[5] = sib[5] + half_x[1]
    for h in (0, 1):
        go(
            lambda h=h: to_x(
                1 if h == 0 else 3,
                sib.at[pl.ds(0 if h == 0 else 4, 2)], full_x.at[h], rs_s.at[22 + h], rs_r.at[22 + h],
            )
        )
    stage2(2)
    stage3(3)
    stage3(2)
    halves_of(terms0, slot(2, 0), True, lambda h: half_a.at[h], 16)
    plus, minus = slot(1, 0), slot(3, 0)
    meet(terms0, plus, minus, lambda h: half_a.at[h], 16)
    fulls_of(terms0, plus, minus, True, lambda h: full_a.at[h], 16)

    loss = loss_out[0, 0]
    for k in range(16):
        for c in (0, 1):
            if k == 0 and c == 0:
                continue
            ref = loss_in.at[c, k]
            to(dev(0, 0, 1), ref, ref, loss_s.at[c * 16 + k], loss_r.at[c * 16 + k]).wait_recv()
            loss = loss + loss_in[c, k]
    loss_ref[...] = loss

    for h in (0, 1):
        got(lambda h: full_a.at[h], h, 18 + h)
    feat_ref[...] = terms0[0].astype(F32) + full_a[0].astype(F32) + full_a[1].astype(F32)

    for h in (0, 1):
        to_x(1, full_x.at[h], full_x.at[h], rs_s.at[22 + h], rs_r.at[22 + h]).wait_recv()
    for h in (0, 1):
        at = pl.ds(pl.multiple_of(mx * 512 + h * 256, 256), 256)
        weight_ref[h * 256 : h * 256 + 256, :] = (
            total[at, :] + full_x[0, h].astype(F32) + full_x[1, h].astype(F32)
        ).astype(BF)

    for make in sent:
        make().wait_send()


def shards(queries_in, classifier, owner_ids, local_ids, targets):
    rows, width = queries_in.shape
    top = owner_ids.shape[1]
    pairs = rows * top
    hot = owner_ids[:, :, None] == jnp.arange(32, dtype=jnp.int32)[None, None, :]
    hit = jnp.any(hot, axis=1)
    before = jnp.tril(jnp.ones((rows, rows), BF), -1)
    rank = jnp.dot(before, hit.astype(BF), preferred_element_type=F32)
    ranks = jnp.sum(jnp.where(hot, rank[:, None, :], 0.0), axis=2).astype(jnp.int32)
    slots = jnp.where(hit, rank + 1.0, 0.0).T.reshape(32, 2, 128)
    tail = jnp.pad(slots, ((0, 0), (1, 13), (0, 0)))
    ids = jnp.broadcast_to((local_ids + 1).reshape(pairs, 1), (pairs, 128))
    labels_in = jnp.concatenate([targets.reshape(pairs, 128), ids], axis=1).astype(BF)
    vmem = pl.BlockSpec(memory_space=pltpu.VMEM)
    block = (rows, width)
    loss, feat, weight = pl.pallas_call(
        kernel,
        out_shape=(
            jax.ShapeDtypeStruct((8, rows), F32),
            jax.ShapeDtypeStruct(block, F32),
            jax.ShapeDtypeStruct((512, width), BF),
        ),
        in_specs=[vmem] * 7,
        out_specs=(vmem, vmem, vmem),
        scratch_shapes=[
            pltpu.VMEM((16, *block), BF),
            pltpu.VMEM((16, *block), BF),
            pltpu.VMEM((32, PAY, 128), BF),
            pltpu.VMEM((2, 16, PAY, 128), BF),
            pltpu.VMEM((16, *block), BF),
            pltpu.VMEM((4, *block), BF),
            pltpu.VMEM((16, *block), BF),
            pltpu.VMEM((4, 2, 128, width), BF),
            pltpu.VMEM((4, 2, *block), BF),
            pltpu.VMEM((2, 128, width), BF),
            pltpu.VMEM((2, *block), BF),
            pltpu.VMEM((2048, width), F32),
            pltpu.VMEM((2, 256, width), BF),
            pltpu.VMEM((2, 2, 256, width), BF),
            pltpu.VMEM((2, 256, width), BF),
            pltpu.VMEM((2, 2048, 256), BF),
            pltpu.VMEM((2, 16, 8, rows), F32),
            pltpu.VMEM((2, 16, 8, rows), F32),
            pltpu.SemaphoreType.DMA((64,)),
            pltpu.SemaphoreType.DMA((32,)),
            pltpu.SemaphoreType.DMA((16,)),
            pltpu.SemaphoreType.DMA((16,)),
            pltpu.SemaphoreType.DMA((32,)),
            pltpu.SemaphoreType.DMA((32,)),
            pltpu.SemaphoreType.DMA((16,)),
            pltpu.SemaphoreType.DMA((16,)),
            pltpu.SemaphoreType.DMA((24,)),
            pltpu.SemaphoreType.DMA((24,)),
            pltpu.SemaphoreType.DMA((32,)),
            pltpu.SemaphoreType.DMA((32,)),
        ],
        compiler_params=pltpu.CompilerParams(
            collective_id=0, has_side_effects=True, vmem_limit_bytes=64 * 1024 * 1024 - 65536
        ),
    )(
        queries_in, classifier, classifier.T, labels_in,
        owner_ids.reshape(1, pairs), ranks.reshape(1, pairs), tail,
    )
    return loss[0], feat, weight


def solution(mesh):
    in_specs = (
        P(("queries", "labels"), None),
        P("labels", None),
        P(("queries", "labels"), None),
        P(("queries", "labels"), None),
        P(("queries", "labels"), None, None),
    )
    out_specs = (
        P(("queries", "labels")),
        P(("queries", "labels"), None),
        P(("labels", "queries"), None),
    )
    return jax.shard_map(shards, mesh=mesh, in_specs=in_specs, out_specs=out_specs, check_vma=False)
```

time: 482 us -> 168 us (0.35); the launches traced: 474 us -> 168 us
  waiting for transfers between devices: 169 us -> 0 us
  Pallas kernels: 0 us -> 151 us
  local copies, waits for them, and re-layouts: 139 us -> 11 us
  matrix products: 77.5 us -> 0.23 us
  other arithmetic: 44.2 us -> 4.76 us
  starting transfers between devices: 29.3 us -> 0 us
  between operations: 14.5 us -> 0.71 us
    all_to_all x5 -> x0, waiting for transfers between devices: 169 us -> none  [the longest x1 75.9 us: shards(): lax.all_to_all(feature_terms.reshape(groups, capacity, feature_width), 'l...]
    pallas_call x0 -> x1, Pallas kernels: none -> 151 us  [shards(): pl.pallas_call(kernel, out_shape=(jax.ShapeDtypeStruct((8, rows), F32), j...]
    dot_general x4 -> x1, matrix products: 77.5 us -> 0.23 us  [shards(): rank = jnp.dot(before, hit.astype(BF), preferred_element_type=F32)]
    gather x5 -> x0, local copies, waits for them, and re-layouts: 66.3 us -> none  [the longest x1 23.3 us: shards(): feature_terms = tile_terms.reshape(padded_row_total, feature_width)[reading]]
    scatter x4 -> x0, local copies, waits for them, and re-layouts: 57.6 us -> none  [the longest x2 35.2 us: to_tiles(): jnp.zeros((padded_row_total, width), rows.dtype).at[position]]
    all_to_all x5 -> x0, starting transfers between devices: 29.3 us -> none  [the longest x1 8.42 us: shards(): lax.all_to_all(sent_ids.reshape(groups, capacity), 'labels', split_axis=0...]
    another operation x8 -> x1, other arithmetic: 25 us -> 0.7 us
    dot_general x1 -> x0, local copies, waits for them, and re-layouts: 9.13 us -> none  [shards(): jnp.einsum('vi,vyf->iyf', tile_onehot_mask, tile_partial_sum, precision=l...]
  transfers between devices with their start and end apart: 6 -> 0, of which waited for: 4 -> 0; matrix products, arithmetic and copies ran while one was open for 18% -> 0% of each run, Pallas kernels for 0% -> 0%
where the time goes in v1:
time: 168 us
  Pallas kernels  151 us (90%)
  local copies, waits for them, and re-layouts  11 us (7%)
  other arithmetic  4.76 us (3%)
    pallas_call x1, Pallas kernels, shards(): pl.pallas_call(kernel, out_shape=(jax.ShapeDtypeStruct((8, rows), F32), j...  151 us
    unnamed x8, local copies, waits for them, and re-layouts  6.75 us

profile of v1, /device:TPU:0, one launch (start us, length us, event | category | flops | bytes accessed | tf_op | source)
XLA Modules:
  0.0 168.0 jit_solution(10770395354349497098)
XLA Ops:
  0.6 0.7 add_convert_fusion
  1.3 0.7 fusion
  2.1 0.2 fusion.2
  2.3 0.8 select_reduce_fusion
  3.1 0.1 copy.18
  3.3 0.1 reshape.35
  3.4 0.1 copy.20
  3.5 0.7 convert_element_type.18.rank_ref
  4.2 0.8 copy.19
  5.1 0.7 reshape.33.owner_ref
  5.8 0.7 pad.4.tail_ref
  6.5 0.0 copy-start
  6.5 0.3 broadcast_in_dim.34
  6.8 1.4 convert_bitcast_fusion
  8.3 1.1 pad_maximum_fusion.labels_in
  9.4 0.0 copy-done
  9.4 3.0 %copy.17 = bf16[2048,768]{0,1:T(8,128)(2,1)} copy(bf16[2048,768]{1,0:T(8,128)(2,1)S(1)} %copy-done) | data formatting | bytes 6291456 | tf_op args[1]
  12.4 151.3 %shard_map.76 = (f32[8,256]{1,0:T(8,128)}, f32[256,768]{1,0:T(8,128)}, bf16[512,768]{1,0:T(8,128)(2,1)}) custom-call(bf16[256,768]{1,0:T(8,128)(2,1)} %q_ref.1, bf16[2048,768]{1,0:T(8,128)(2,1)} %w.1, bf16[768,2048]{1,0:T(8,128)(2,1)} %bitcast.7, bf16[2048,256]{1,0:T(8,128)(2,1)} %pad_maximum_fusion.labels_in, s32[1,2048]{1,0:T(1,128)} %reshape.33.owner_ref, ...), custom_call_target="tpu_custom_call" | custom-call | tf_op jit(solution)/shard_map/pallas_call | solution.py:405
  163.7 0.0 copy-start.1
  163.7 1.3 slice.3
  165.0 2.1 %copy.23 = f32[256,768]{1,0:T(8,128)} copy(f32[256,768]{1,0:T(8,128)} %get-tuple-element.13) | data formatting | bytes 1572864
  167.1 0.0 copy-done.1
  167.1 0.9 copy.24
  (4 shorter events, 0.0 us)
Async XLA Ops:
  6.5 2.9 %copy-start = (bf16[2048,768]{1,0:T(8,128)(2,1)S(1)}, bf16[2048,768]{1,0:T(8,128)(2,1)}, u32[]{:S(2)}) copy-start(bf16[2048,768]{1,0:T(8,128)(2,1)} %w.1) | copy-start | bytes 9437188
  163.7 3.4 %copy-start.1 = (bf16[512,768]{1,0:T(8,128)(2,1)S(1)}, bf16[512,768]{1,0:T(8,128)(2,1)}, u32[]{:S(2)}) copy-start(bf16[512,768]{1,0:T(8,128)(2,1)} %get-tuple-element.14) | copy-start | bytes 2359300

commit v2 on v1

--- a/solution.py
+++ b/solution.py
@@ -30,20 +30,26 @@
     return jnp.dot(a, b, preferred_element_type=F32)
 
 
-def one_chunk(k, own, sib, pay, w, wt, rows, grads, terms0, terms1, loss_out):
-    half = lax.rem(k, 2)
+def tn(a, b):
+    return lax.dot_general(a, b, (((0,), (0,)), ((), ())), preferred_element_type=F32)
+
+
+def pick_of(pay, core, k):
     spot = lax.broadcasted_iota(jnp.int32, (128, 128), 0).astype(F32) + 1.0
-    picks, ids = [], []
+    tail = pay[core, k, 128:144, :].astype(F32)
+    return jnp.concatenate(
+        [jnp.where(spot == tail[r : r + 1, :], 1.0, 0.0) for r in (1, 2)], axis=1
+    ).astype(BF)
+
+
+def make_grads(k, own, sib, pay, w, rows, grads, loss_out):
+    picks = [pick_of(pay, core, k) for core in (0, 1)]
     for core, src in enumerate((own, sib)):
-        tail = pay[core, k, 128:144, :].astype(F32)
-        ids.append(tail[0:1, :])
-        pick = jnp.concatenate(
-            [jnp.where(spot == tail[r : r + 1, :], 1.0, 0.0) for r in (1, 2)], axis=1
-        )
-        picks.append(pick)
-        rows[half, core * 128 : core * 128 + 128, :] = nn(pick.astype(BF), src[k]).astype(BF)
-    ids = jnp.concatenate(ids, axis=1)
-    x = rows[half]
+        rows[core * 128 : core * 128 + 128, :] = nn(picks[core], src[k]).astype(BF)
+    ids = jnp.concatenate(
+        [pay[core, k, 128:144, :].astype(F32)[0:1, :] for core in (0, 1)], axis=1
+    )
+    x = rows[...]
     z = jnp.zeros((128, 256), F32)
     for part in range(2):
         scores = nt(w[part * 1024 : part * 1024 + 1024, :], x)
@@ -55,39 +61,42 @@
     e = jnp.exp(-jnp.abs(z))
     loss = jnp.sum(jnp.maximum(z, 0.0) + jnp.log1p(e) - y * z, axis=0, keepdims=True) * valid
     sig = jnp.where(z >= 0.0, 1.0, e) / (1.0 + e)
-    g = (sig - y) * valid
+    g = ((sig - y) * valid).astype(BF).reshape(8, 16, 256)
+    many = jnp.broadcast_to(ids, (16, 256))
     for b in range(16):
-        grads[half, b * 128 : b * 128 + 128, :] = jnp.where(ids == float(b + 1), g, 0.0).astype(BF)
-    ft = nn(wt[...], grads[half]).astype(BF)
+        hot = jnp.where(many == float(b + 1), 1.0, 0.0).astype(BF)
+        grads[b * 128 : b * 128 + 128, :] = (g * hot[None]).reshape(128, 256)
     place = lax.broadcasted_iota(jnp.int32, (16, 128), 0)
-    for core, terms in enumerate((terms0, terms1)):
-        index = k if core == 0 else lax.rem(k, 4)
-        pick = picks[core]
-        terms[index] = nt(pick.T.astype(BF), ft[:, core * 128 : core * 128 + 128]).astype(BF)
+    for core in (0, 1):
         part = loss[:, core * 128 : core * 128 + 128]
         high = part.astype(BF).astype(F32)
         mid = (part - high).astype(BF).astype(F32)
         low = part - high - mid
         stack = jnp.where(place == 0, high, jnp.where(place == 1, mid, jnp.where(place == 2, low, 0.0)))
-        spread = nn(stack.astype(BF), pick.astype(BF))
+        spread = nn(stack.astype(BF), picks[core])
         loss_out[core, k] = jnp.broadcast_to(jnp.sum(spread, axis=0, keepdims=True), (8, 256))
 
 
-def add_weight(rows, grads, total):
-    def step(m, _):
-        at = pl.ds(pl.multiple_of(m * 512, 512), 512)
-        total[at, :] += nn(grads[0, at, :], rows[0]) + nn(grads[1, at, :], rows[1])
-        return 0
-
-    lax.fori_loop(0, 4, step, 0)
+def make_terms(k, pay, w, grads, terms0, terms1, index):
+    f = tn(grads[...], w[...]).astype(BF)
+    terms0[k] = tn(pick_of(pay, 0, k), f[0:128, :]).astype(BF)
+    terms1[index] = tn(pick_of(pay, 1, k), f[128:256, :]).astype(BF)
+
+
+def add_weight(part, rows, grads, total):
+    at = slice(part * 1024, part * 1024 + 1024)
+    left = jnp.concatenate([grads[0][at, :], grads[1][at, :]], axis=1)
+    right = jnp.concatenate([rows[0][...], rows[1][...]], axis=0)
+    total[at, :] += nn(left, right)
 
 
 def kernel(
-    q_ref, w, wt, labels_in, owner_ref, rank_ref, tail_ref,
+    q_ref, w, targets, owner_ref, local_ref,
     loss_ref, feat_ref, weight_ref,
     own, sib, pay_out, pay, terms0, terms1, back, half_in, full_in, half_a, full_a,
-    total, half_x, full_x, rows, grads, loss_out, loss_in,
-    own_s, own_r, sib_s, sib_r, pay_s, pay_r, back_s, back_r, rs_s, rs_r, loss_s, loss_r,
+    total, half_x, full_x, rows0, rows1, rows2, rows3, grads0, grads1, grads2, grads3,
+    loss_out, loss_in, labels_in, slots,
+    own_s, own_r, sib_s, sib_r, pay_s, pay_r, back_s, back_r, rs_s, rs_r, loss_s, loss_r, known,
 ):
     me = lax.axis_index("labels")
     mx = lax.axis_index("queries")
@@ -113,19 +122,23 @@
         )
 
     barrier = pltpu.get_barrier_semaphore()
-
-    def greet(i, _):
-        pl.semaphore_signal(
-            barrier, inc=1, device_id={"labels": lax.rem(me + i, 32)}, device_id_type=MESH
-        )
-        return 0
-
-    lax.fori_loop(1, 32, greet, 0)
+    ring_a, ring_b = (dev(1, 0), dev(3, 0)), (dev(0, 1), dev(0, 3))
+    for device in (*ring_a, *ring_b, dev(0, 0, 1)):
+        pl.semaphore_signal(barrier, inc=1, device_id={"labels": device}, device_id_type=MESH)
     for step in (1, 3):
         pl.semaphore_signal(
             barrier, inc=1, device_id={"queries": lax.rem(mx + step, 4)}, device_id_type=MESH
         )
-    pl.semaphore_wait(barrier, 33)
+    pl.semaphore_wait(barrier, 7)
+
+    def tell(index, devices):
+        for device in devices:
+            pl.semaphore_signal(
+                known.at[index], inc=1, device_id={"labels": device}, device_id_type=MESH
+            )
+
+    def hear(index, count):
+        pl.semaphore_wait(known.at[index], count)
 
     sent = []
 
@@ -175,29 +188,68 @@
     own[0] = q_ref[...]
     pass_on(0)
 
-    spot = lax.broadcasted_iota(jnp.int32, (128, 2048), 0)
-    first = lax.broadcasted_iota(jnp.int32, (16, 128), 0) == 0
+    tell(0, ring_a)
+    lane = lax.broadcasted_iota(jnp.int32, (256, 128), 1)
+    hit = jnp.zeros((256, 128), F32)
+    owners = jnp.zeros((256, 128), F32)
+    for t in range(8):
+        named = jnp.broadcast_to(owner_ref[:, t : t + 1], (256, 128))
+        hit = jnp.where(lane == named, 1.0, hit)
+        owners = jnp.where(lane == t, named.astype(F32), owners)
+        at = slice(t * 256, t * 256 + 256)
+        labels_in[at, 0:128] = targets[pl.ds(t, 256, stride=8), :].astype(BF)
+        labels_in[at, 128:256] = (
+            jnp.broadcast_to(local_ref[:, t : t + 1], (256, 128)) + 1
+        ).astype(F32).astype(BF)
+    before = jnp.where(
+        lax.broadcasted_iota(jnp.int32, (256, 256), 1) < lax.broadcasted_iota(jnp.int32, (256, 256), 0),
+        1.0, 0.0,
+    )
+    rank = nn(before.astype(BF), hit.astype(BF))
+    slots[...] = jnp.where(hit > 0.5, rank + 1.0, 0.0).T
+    owners = owners.T[0:8, :]
+    hear(0, 2)
+    tell(1, ring_b)
+    spot = lax.broadcasted_iota(jnp.int32, (128, 256), 0).astype(F32) + 1.0
+    place = lax.broadcasted_iota(jnp.int32, (16, 128), 0)
 
     def pack(group, _):
-        owners = owner_ref[...]
-        ranks = rank_ref[...]
-        stack = jnp.concatenate(
-            [
-                jnp.where(spot == jnp.where(owners == group * 4 + i, ranks, -1), 1.0, 0.0).astype(BF)
-                for i in range(4)
-            ],
-            axis=0,
-        )
-        found = nn(stack, labels_in[...])
+        stacks = []
         for i in range(4):
+            o = group * 4 + i
+            mine = slots[pl.ds(o, 1), :]
+            stacks.append(
+                jnp.concatenate(
+                    [
+                        jnp.where(
+                            spot == jnp.where(owners[t : t + 1, :] == o.astype(F32), mine, 0.0), 1.0, 0.0
+                        ).astype(BF)
+                        for t in range(8)
+                    ],
+                    axis=1,
+                )
+            )
+        found = nn(jnp.concatenate(stacks, axis=0), labels_in[...])
+        for i in range(4):
+            o = group * 4 + i
             piece = found[i * 128 : i * 128 + 128, :]
-            o = group * 4 + i
             pay_out[o, 0:128, :] = piece[:, 0:128].T.astype(BF)
             ids = piece[:, 128:256].T[0:16, :]
-            pay_out[o, 128:144, :] = (jnp.where(first, ids, 0.0) + tail_ref[o]).astype(BF)
+            mine = slots[pl.ds(o, 1), :]
+            tail = jnp.where(
+                place == 0, ids,
+                jnp.where(place == 1, mine[:, 0:128], jnp.where(place == 2, mine[:, 128:256], 0.0)),
+            )
+            pay_out[o, 128:144, :] = tail.astype(BF)
         return 0
 
-    lax.fori_loop(0, 8, pack, 0)
+    lax.fori_loop(0, 4, pack, 0)
+    hear(1, 2)
+    tell(2, ring_b)
+    lax.fori_loop(4, 8, pack, 0)
+    hear(2, 2)
+    tell(3, (dev(0, 0, 1),))
+    hear(3, 1)
     pay[0, 0] = pay_out[me]
     for k, (a, b) in enumerate(ORDER):
         for c in (0, 1):
@@ -267,52 +319,75 @@
         3: [lambda: [arrive(k) for k in (5, 6)]],
         4: [lambda: [arrive(k) for k in (7, 8, 9, 12)]],
         6: [lambda: [arrive(k) for k in (10, 11, 13, 14)]],
-        8: [lambda: stage1(0)],
-        9: [lambda: arrive(15)],
-        10: [lambda: stage2(0)],
-        12: [lambda: stage3(0)],
-        13: [lambda: stage1(1)],
-        14: [lambda: stage2(1)],
-        15: [lambda: stage3(1), lambda: stage1(3)],
+        8: [lambda: arrive(15)],
+        9: [lambda: stage1(0)],
+        11: [lambda: stage2(0)],
+        13: [lambda: stage3(0)],
+        14: [lambda: stage1(1)],
+        15: [lambda: stage2(1)],
     }
 
     def send_back(k, index):
         return to(dev(0, 0, 1), terms1.at[index], back.at[k], back_s.at[k], back_r.at[k])
 
-    total[...] = jnp.zeros_like(total)
-
-    def step(k, _):
-        for when, todo in acts.items():
-
-            @pl.when(k == when)
-            def _():
-                for act in todo:
-                    act()
-
-        to(dev(0, 0, 1), sib.at[k], sib.at[k], sib_s.at[k], sib_r.at[k]).wait_recv()
-
-        @pl.when(k > 0)
-        def _():
-            to(dev(0, 0, 1), pay.at[0, k], pay.at[0, k], pay_s.at[k], pay_r.at[k]).wait_recv()
-
-        to(dev(0, 0, 1), pay.at[1, k], pay.at[1, k], pay_s.at[16 + k], pay_r.at[16 + k]).wait_recv()
-
-        @pl.when(k >= 4)
-        def _():
-            send_back(k - 4, lax.rem(k, 4)).wait_send()
-
-        one_chunk(k, own, sib, pay, w, wt, rows, grads, terms0, terms1, loss_out)
-        send_back(k, lax.rem(k, 4)).start()
-
-        @pl.when(lax.rem(k, 2) == 1)
-        def _():
-            add_weight(rows, grads, total)
-
+    all_rows = (rows0, rows1, rows2, rows3)
+    all_grads = (grads0, grads1, grads2, grads3)
+    for ref in (*all_rows[2:], *all_grads[2:], total):
+        ref[...] = jnp.zeros_like(ref)
+
+    def step(j, _):
+        for i in range(4):
+            k = j * 4 + i
+            for when, todo in acts.items():
+                if when % 4 != i:
+                    continue
+
+                @pl.when(j == when // 4)
+                def _():
+                    for act in todo:
+                        act()
+
+            to(dev(0, 0, 1), sib.at[k], sib.at[k], sib_s.at[k], sib_r.at[k]).wait_recv()
+            to(dev(0, 0, 1), pay.at[1, k], pay.at[1, k], pay_s.at[16 + k], pay_r.at[16 + k]).wait_recv()
+
+            def mine():
+                to(dev(0, 0, 1), pay.at[0, k], pay.at[0, k], pay_s.at[k], pay_r.at[k]).wait_recv()
+
+            if i == 0:
+                pl.when(j > 0)(mine)
+            else:
+                mine()
+
+            last = (i - 1) % 4
+            if i == 0:
+
+                @pl.when(j > 1)
+                def _():
+                    send_back(k - 5, last).wait_send()
+
+            else:
+
+                @pl.when(j > 0)
+                def _():
+                    send_back(k - 5, last).wait_send()
+
+            pair = 2 if i < 2 else 0
+            make_grads(k, own, sib, pay, w, all_rows[i], all_grads[i], loss_out)
+            make_terms(k - 1 + lax.div(16 - k, 16), pay, w, all_grads[last], terms0, terms1, last)
+            add_weight(i % 2, all_rows[pair : pair + 2], all_grads[pair : pair + 2], total)
+            if i == 0:
+
+                @pl.when(j > 0)
+                def _():
+                    send_back(k - 1, last).start()
+
+            else:
+                send_back(k - 1, last).start()
         return 0
 
-    lax.fori_loop(0, 16, step, 0)
-    for k in range(12, 16):
-        send_back(k, k % 4).wait_send()
+    lax.fori_loop(0, 4, step, 0)
+    for part in (0, 1):
+        add_weight(part, all_rows[2:], all_grads[2:], total)
 
     def shard(dx):
         return pl.ds(pl.multiple_of(lax.rem(mx + dx, 4) * 512, 512), 512)
@@ -328,6 +403,11 @@
                         1 if h == 0 else 3, sib.at[2 + h], half_x.at[h], rs_s.at[20 + h], rs_r.at[20 + h]
                     )
                 )
+    send_back(11, 3).wait_send()
+    make_terms(15, pay, w, grads3, terms0, terms1, 3)
+    send_back(15, 3).start()
+    stage3(1)
+    stage1(3)
     stage1(2)
 
     for k, (a, b) in enumerate(ORDER):
@@ -383,6 +463,8 @@
             total[at, :] + full_x[0, h].astype(F32) + full_x[1, h].astype(F32)
         ).astype(BF)
 
+    for k in range(12, 16):
+        send_back(k, k % 4).wait_send()
     for make in sent:
         make().wait_send()
 
@@ -391,15 +473,6 @@
     rows, width = queries_in.shape
     top = owner_ids.shape[1]
     pairs = rows * top
-    hot = owner_ids[:, :, None] == jnp.arange(32, dtype=jnp.int32)[None, None, :]
-    hit = jnp.any(hot, axis=1)
-    before = jnp.tril(jnp.ones((rows, rows), BF), -1)
-    rank = jnp.dot(before, hit.astype(BF), preferred_element_type=F32)
-    ranks = jnp.sum(jnp.where(hot, rank[:, None, :], 0.0), axis=2).astype(jnp.int32)
-    slots = jnp.where(hit, rank + 1.0, 0.0).T.reshape(32, 2, 128)
-    tail = jnp.pad(slots, ((0, 0), (1, 13), (0, 0)))
-    ids = jnp.broadcast_to((local_ids + 1).reshape(pairs, 1), (pairs, 128))
-    labels_in = jnp.concatenate([targets.reshape(pairs, 128), ids], axis=1).astype(BF)
     vmem = pl.BlockSpec(memory_space=pltpu.VMEM)
     block = (rows, width)
     loss, feat, weight = pl.pallas_call(
@@ -409,7 +482,7 @@
             jax.ShapeDtypeStruct(block, F32),
             jax.ShapeDtypeStruct((512, width), BF),
         ),
-        in_specs=[vmem] * 7,
+        in_specs=[vmem] * 5,
         out_specs=(vmem, vmem, vmem),
         scratch_shapes=[
             pltpu.VMEM((16, *block), BF),
@@ -426,10 +499,12 @@
             pltpu.VMEM((2048, width), F32),
             pltpu.VMEM((2, 256, width), BF),
             pltpu.VMEM((2, 2, 256, width), BF),
-            pltpu.VMEM((2, 256, width), BF),
-            pltpu.VMEM((2, 2048, 256), BF),
+            *[pltpu.VMEM((256, width), BF)] * 4,
+            *[pltpu.VMEM((2048, 256), BF)] * 4,
             pltpu.VMEM((2, 16, 8, rows), F32),
             pltpu.VMEM((2, 16, 8, rows), F32),
+            pltpu.VMEM((pairs, 256), BF),
+            pltpu.VMEM((128, rows), F32),
             pltpu.SemaphoreType.DMA((64,)),
             pltpu.SemaphoreType.DMA((32,)),
             pltpu.SemaphoreType.DMA((16,)),
@@ -442,13 +517,13 @@
             pltpu.SemaphoreType.DMA((24,)),
             pltpu.SemaphoreType.DMA((32,)),
             pltpu.SemaphoreType.DMA((32,)),
+            pltpu.SemaphoreType.REGULAR((4,)),
         ],
         compiler_params=pltpu.CompilerParams(
             collective_id=0, has_side_effects=True, vmem_limit_bytes=64 * 1024 * 1024 - 65536
         ),
     )(
-        queries_in, classifier, classifier.T, labels_in,
-        owner_ids.reshape(1, pairs), ranks.reshape(1, pairs), tail,
+        queries_in, classifier, targets.reshape(pairs, 128), owner_ids, local_ids,
     )
     return loss[0], feat, weight
 

time: 168 us -> 147 us (0.88)
  Pallas kernels: 151 us -> 138 us
  other arithmetic: 4.76 us -> 0 us
  local copies, waits for them, and re-layouts: 11 us -> 8.35 us
    pallas_call x1, Pallas kernels: 151 us -> 138 us  [shards(): pl.pallas_call(kernel, out_shape=(jax.ShapeDtypeStruct((8, rows), F32), j...]
    unnamed x8 -> x4, local copies, waits for them, and re-layouts: 6.75 us -> 7.09 us
where the time goes in v2:
time: 147 us
  Pallas kernels  138 us (94%)
  local copies, waits for them, and re-layouts  8.35 us (6%)
    pallas_call x1, Pallas kernels, shards(): pl.pallas_call(kernel, out_shape=(jax.ShapeDtypeStruct((8, rows), F32), j...  138 us
    unnamed x4, local copies, waits for them, and re-layouts  7.09 us

profile of v2, /device:TPU:0, one launch (start us, length us, event | category | flops | bytes accessed | tf_op | source)
XLA Modules:
  0.0 146.9 jit_solution(8401848569045738119)
XLA Ops:
  0.6 1.5 %copy.8.owner_ref = s32[256,8]{1,0:T(8,128)} copy(s32[256,8]{0,1:T(8,128)} %param.7) | data formatting | bytes 16384 | tf_op args[2]
  2.1 1.5 %copy.9.local_ref = s32[256,8]{1,0:T(8,128)} copy(s32[256,8]{0,1:T(8,128)} %param.8) | data formatting | bytes 16384 | tf_op args[3]
  3.6 138.0 %shard_map.76 = (f32[8,256]{1,0:T(8,128)}, f32[256,768]{1,0:T(8,128)}, bf16[512,768]{1,0:T(8,128)(2,1)}) custom-call(bf16[256,768]{1,0:T(8,128)(2,1)} %q_ref.1, bf16[2048,768]{1,0:T(8,128)(2,1)} %w.1, s32[2048,128]{1,0:T(8,128)} %bitcast.2, s32[256,8]{1,0:T(8,128)} %copy.8.owner_ref, s32[256,8]{1,0:T(8,128)} %copy.9.local_ref), custom_call_target="tpu_custom_call" | custom-call | tf_op jit(solution)/shard_map/pallas_call | solution.py:478
  141.6 1.3 slice.3
  142.8 2.1 %copy.12 = f32[256,768]{1,0:T(8,128)} copy(f32[256,768]{1,0:T(8,128)} %get-tuple-element.13) | data formatting | bytes 1572864
  144.9 2.1 %copy.13 = bf16[512,768]{1,0:T(8,128)(2,1)} copy(bf16[512,768]{1,0:T(8,128)(2,1)} %get-tuple-element.14) | data formatting | bytes 1572864

commit v3 on v2

v3 whole, which is shorter than its diff:
```python
import jax
import jax.numpy as jnp
from jax import lax
from jax.experimental import pallas as pl
from jax.experimental.pallas import tpu as pltpu
from jax.sharding import PartitionSpec as P

MESH = pl.DeviceIdType.MESH
BF = jnp.bfloat16
F32 = jnp.float32

ORDER = [
    (0, 0), (0, 1), (1, 0), (0, 2), (2, 0), (1, 1), (1, 3), (3, 1),
    (3, 3), (2, 1), (1, 2), (2, 3), (3, 2), (2, 2), (0, 3), (3, 0),
]
SLOT = {chip: k for k, chip in enumerate(ORDER)}
MIRROR = [SLOT[(b, a)] for a, b in ORDER]
PAY = 144


def slot(a, b):
    return SLOT[(a % 4, b % 4)]


def nt(a, b):
    return lax.dot_general(a, b, (((1,), (1,)), ((), ())), preferred_element_type=F32)


def nn(a, b):
    return jnp.dot(a, b, preferred_element_type=F32)


def tn(a, b):
    return lax.dot_general(a, b, (((0,), (0,)), ((), ())), preferred_element_type=F32)


def pick_of(pay, core, k):
    spot = lax.broadcasted_iota(jnp.int32, (128, 128), 0).astype(F32) + 1.0
    tail = pay[core, k, 128:144, :].astype(F32)
    return jnp.concatenate(
        [jnp.where(spot == tail[r : r + 1, :], 1.0, 0.0) for r in (1, 2)], axis=1
    ).astype(BF)


def make_grads(k, own, sib, pay, w, grads, g_all, ids_all, loss_out):
    picks = [pick_of(pay, core, k) for core in (0, 1)]
    x = jnp.concatenate(
        [nn(picks[core], src[k]).astype(BF) for core, src in enumerate((own, sib))], axis=0
    )
    sib[k] = x
    ids = jnp.concatenate(
        [pay[core, k, 128:144, :].astype(F32)[0:1, :] for core in (0, 1)], axis=1
    )
    z = jnp.zeros((128, 256), F32)
    for part in range(2):
        scores = nt(w[part * 1024 : part * 1024 + 1024, :], x)
        for b in range(8):
            z = jnp.where(ids == float(part * 8 + b + 1), scores[b * 128 : b * 128 + 128, :], z)
    z = z.astype(BF).astype(F32)
    y = jnp.concatenate([pay[core, k, 0:128, :] for core in (0, 1)], axis=1).astype(F32)
    valid = jnp.where(ids > 0.5, 0.25, 0.0)
    e = jnp.exp(-jnp.abs(z))
    loss = jnp.sum(jnp.maximum(z, 0.0) + jnp.log1p(e) - y * z, axis=0, keepdims=True) * valid
    sig = jnp.where(z >= 0.0, 1.0, e) / (1.0 + e)
    g = ((sig - y) * valid).astype(BF)
    many = jnp.broadcast_to(ids, (16, 256))
    g_all[k] = g
    ids_all[k] = many
    g = g.reshape(8, 16, 256)
    for b in range(16):
        hot = jnp.where(many == float(b + 1), 1.0, 0.0).astype(BF)
        grads[b * 128 : b * 128 + 128, :] = (g * hot[None]).reshape(128, 256)
    place = lax.broadcasted_iota(jnp.int32, (16, 128), 0)
    for core in (0, 1):
        part = loss[:, core * 128 : core * 128 + 128]
        high = part.astype(BF).astype(F32)
        mid = (part - high).astype(BF).astype(F32)
        low = part - high - mid
        stack = jnp.where(place == 0, high, jnp.where(place == 1, mid, jnp.where(place == 2, low, 0.0)))
        spread = nn(stack.astype(BF), picks[core])
        loss_out[core, k] = jnp.broadcast_to(jnp.sum(spread, axis=0, keepdims=True), (8, 256))


def make_terms(k, pay, w, grads, terms0, terms1, index):
    f = tn(grads[...], w[...]).astype(BF)
    terms0[k] = tn(pick_of(pay, 0, k), f[0:128, :]).astype(BF)
    terms1[index] = tn(pick_of(pay, 1, k), f[128:256, :]).astype(BF)


def weight_shard(first, count, sib, g_all, ids_all, wide, total):
    def step(j, _):
        for i in range(4):
            k = j * 4 + i
            many = ids_all[k]
            g = g_all[k].reshape(8, 16, 256)
            for b in range(count):
                hot = jnp.where(many == (first + (b + 1)).astype(F32), 1.0, 0.0).astype(BF)
                wide[b * 128 : b * 128 + 128, i * 256 : i * 256 + 256] = (g * hot[None]).reshape(128, 256)
        size = count * 128
        x = sib[pl.ds(j * 4, 4)].reshape(1024, 768)
        total[0:size, :] += nn(wide[0:size, :], x)
        return 0

    total[...] = jnp.zeros_like(total)
    lax.fori_loop(0, 4, step, 0)


def kernel(
    q_ref, w, targets, owner_ref, local_ref,
    loss_ref, feat_ref, weight_ref,
    own, sib, pay_out, pay, terms0, terms1, back, half_in, full_in, half_a, full_a,
    total, half_x, full_x, shards_x, wide, g_all, ids_all, grads0, grads1,
    loss_out, loss_in, labels_in, slots,
    own_s, own_r, sib_s, sib_r, pay_s, pay_r, back_s, back_r, rs_s, rs_r, loss_s, loss_r, x_s, x_r, known,
):
    me = lax.axis_index("labels")
    mx = lax.axis_index("queries")
    core = lax.rem(me, 2)
    my = lax.rem(me // 2, 4)
    mz = me // 8

    def dev(a, b, c=0):
        dz = a * (1 - core) + b * core
        dy = b * (1 - core) + a * core
        return (lax.rem(mz + dz, 4) * 4 + lax.rem(my + dy, 4)) * 2 + lax.rem(core + c, 2)

    def to(device, src, dst, ssem, rsem):
        return pltpu.make_async_remote_copy(
            src_ref=src, dst_ref=dst, send_sem=ssem, recv_sem=rsem,
            device_id={"labels": device}, device_id_type=MESH,
        )

    def to_x(step, src, dst, ssem, rsem):
        return pltpu.make_async_remote_copy(
            src_ref=src, dst_ref=dst, send_sem=ssem, recv_sem=rsem,
            device_id={"queries": lax.rem(mx + step, 4)}, device_id_type=MESH,
        )

    barrier = pltpu.get_barrier_semaphore()
    ring_a, ring_b = (dev(1, 0), dev(3, 0)), (dev(0, 1), dev(0, 3))
    for device in (*ring_a, *ring_b, dev(0, 0, 1)):
        pl.semaphore_signal(barrier, inc=1, device_id={"labels": device}, device_id_type=MESH)
    for step in (1, 3):
        pl.semaphore_signal(
            barrier, inc=1, device_id={"queries": lax.rem(mx + step, 4)}, device_id_type=MESH
        )
    pl.semaphore_wait(barrier, 7)

    def tell(index, devices):
        for device in devices:
            pl.semaphore_signal(
                known.at[index], inc=1, device_id={"labels": device}, device_id_type=MESH
            )

    def hear(index, count):
        pl.semaphore_wait(known.at[index], count)

    sent = []

    def go(make):
        make().start()
        sent.append(make)

    def rows_of(ref, half):
        return ref if half is None else ref.at[pl.ds(half * 128, 128), :]

    def pass_on(*slots):
        sends = []
        for k in slots:
            a, b = ORDER[k]
            if b == 0:
                if a == 0:
                    sends += [(k, 1, 0, None), (k, 3, 0, None)]
                if a == 3:
                    sends.append((k, 1, 0, 0))
                if a == 1:
                    sends.append((k, 3, 0, 1))
                sends += [(k, 0, 1, None), (k, 0, 3, None)]
            if b == 3:
                sends.append((k, 0, 1, 0))
            if b == 1:
                sends.append((k, 0, 3, 1))
        sends.sort(key=lambda send: send[3] is None)
        for n, (k, sa, sb, half) in enumerate(sends):
            a, b = ORDER[k]
            there = slot(a - sa, b - sb)
            index = k * 4 + [send for send in sends if send[0] == k].index((k, sa, sb, half))
            go(
                lambda k=k, sa=sa, sb=sb, half=half, there=there, index=index: to(
                    dev(sa, sb),
                    rows_of(own.at[k], half),
                    rows_of(own.at[there], half),
                    own_s.at[index],
                    own_r.at[there * 2 + (half or 0)],
                )
            )
        for k in slots:
            go(
                lambda k=k: to(
                    dev(0, 0, 1), own.at[k], sib.at[MIRROR[k]], sib_s.at[k], sib_r.at[MIRROR[k]]
                )
            )

    def arrive(*slots):
        for k in slots:
            a, b = ORDER[k]
            halves = (0, 1) if b == 2 or (b == 0 and a == 2) else (None,)
            for half in halves:
                ref = rows_of(own.at[k], half)
                to(dev(0, 0, 1), ref, ref, own_s.at[k * 4], own_r.at[k * 2 + (half or 0)]).wait_recv()
        pass_on(*slots)

    own[0] = q_ref[...]
    pass_on(0)

    tell(0, ring_a)
    owners = owner_ref[...]
    line = lax.broadcasted_iota(jnp.int32, (32, 256), 0)
    hit = jnp.zeros((32, 256), F32)
    for t in range(8):
        hit = jnp.where(line == owners[t : t + 1, :], 1.0, hit)
    before = jnp.where(
        lax.broadcasted_iota(jnp.int32, (256, 256), 0) < lax.broadcasted_iota(jnp.int32, (256, 256), 1),
        1.0, 0.0,
    )
    rank = nn(hit.astype(BF), before.astype(BF))
    slots[...] = jnp.where(hit > 0.5, rank + 1.0, 0.0)
    columns = jnp.concatenate(
        [local_ref[...].astype(F32) + 1.0, jnp.zeros((120, 256), F32)], axis=0
    ).T
    for t in range(8):
        at = slice(t * 256, t * 256 + 256)
        labels_in[at, 0:128] = targets[pl.ds(t, 256, stride=8), :].astype(BF)
        labels_in[at, 128:256] = jnp.broadcast_to(columns[:, t : t + 1], (256, 128)).astype(BF)
    hear(0, 2)
    tell(1, ring_b)
    spot = lax.broadcasted_iota(jnp.int32, (128, 256), 0).astype(F32) + 1.0
    place = lax.broadcasted_iota(jnp.int32, (16, 128), 0)

    def pack(group, _):
        stacks = []
        for i in range(4):
            o = group * 4 + i
            mine = slots[pl.ds(o, 1), :]
            stacks.append(
                jnp.concatenate(
                    [
                        jnp.where(
                            spot == jnp.where(owners[t : t + 1, :] == o, mine, 0.0), 1.0, 0.0
                        ).astype(BF)
                        for t in range(8)
                    ],
                    axis=1,
                )
            )
        found = nn(jnp.concatenate(stacks, axis=0), labels_in[...])
        for i in range(4):
            o = group * 4 + i
            piece = found[i * 128 : i * 128 + 128, :]
            pay_out[o, 0:128, :] = piece[:, 0:128].T.astype(BF)
            ids = piece[:, 128:256].T[0:16, :]
            mine = slots[pl.ds(o, 1), :]
            tail = jnp.where(
                place == 0, ids,
                jnp.where(place == 1, mine[:, 0:128], jnp.where(place == 2, mine[:, 128:256], 0.0)),
            )
            pay_out[o, 128:144, :] = tail.astype(BF)
        return 0

    lax.fori_loop(0, 4, pack, 0)
    hear(1, 2)
    tell(2, ring_b)
    lax.fori_loop(4, 8, pack, 0)
    hear(2, 2)
    tell(3, (dev(0, 0, 1),))
    hear(3, 1)
    pay[0, 0] = pay_out[me]

    def targets_to(wanted):
        for there in wanted:
            for c in (0, 1):
                if there == 0 and c == 0:
                    continue
                a, b = ORDER[there]
                a, b = (-a % 4, -b % 4) if c == 0 else (-b % 4, -a % 4)

                def make(a=a, b=b, c=c, there=there):
                    d = dev(a, b, c)
                    return to(
                        d, pay_out.at[d], pay.at[c, there], pay_s.at[c * 16 + there], pay_r.at[c * 16 + there]
                    )

                go(make)

    def halves_of(buf, index, a_axis, store, sem):
        for h in (0, 1):
            step = 1 if h == 0 else 3
            d = (step, 0) if a_axis else (0, step)
            go(
                lambda d=d, h=h: to(
                    dev(*d), rows_of(buf.at[index], h), store(h), rs_s.at[sem + h], rs_r.at[sem + h]
                )
            )

    def full_of(h, index, a_axis, store, sem):
        step = 1 if h == 0 else 3
        d = (step, 0) if a_axis else (0, step)
        go(
            lambda: to(dev(*d), buf_at(index), store(h), rs_s.at[sem + 2 + h], rs_r.at[sem + 2 + h])
        )

    def buf_at(index):
        return terms0.at[index]

    def got(store, h, sem):
        to(dev(0, 0, 1), store(h), store(h), rs_s.at[sem], rs_r.at[sem]).wait_recv()

    def summed(a, b):
        k = slot(a, b)
        far = MIRROR[k]
        to(dev(0, 0, 1), back.at[far], back.at[far], back_s.at[far], back_r.at[far]).wait_recv()
        terms0[k] = terms0[k] + back[far]

    def far(a):
        summed(a, 2)
        halves_of(terms0, slot(a, 2), False, lambda h: half_in.at[a, h], a * 4)

    def meet(h, index, store, sem):
        got(store, h, sem + h)
        at = slice(h * 128, h * 128 + 128)
        terms0[index, at, :] = terms0[index, at, :] + store(h)[...]

    def near(a, h):
        index = slot(a, 1 if h == 0 else 3)
        summed(a, 1 if h == 0 else 3)
        meet(h, index, lambda h: half_in.at[a, h], a * 4)
        full_of(h, index, False, lambda h: full_in.at[a, h], a * 4)

    def here(a):
        summed(a, 0)
        for h in (0, 1):
            got(lambda h: full_in.at[a, h], h, a * 4 + 2 + h)
        k = slot(a, 0)
        terms0[k] = (
            terms0[k].astype(F32) + full_in[a, 0].astype(F32) + full_in[a, 1].astype(F32)
        ).astype(BF)

    def arrivals(*chips):
        arrive(*[slot(a, b) for a, b in chips])

    acts = {
        0: [lambda: targets_to(range(0, 5)), lambda: arrivals((0, 1), (1, 0), (0, 3), (3, 0))],
        1: [lambda: targets_to(range(5, 8))],
        2: [lambda: targets_to(range(8, 10)), lambda: arrivals((2, 0), (0, 2))],
        3: [lambda: targets_to(range(10, 13))],
        4: [lambda: targets_to(range(13, 16)), lambda: arrivals((1, 1), (1, 3), (3, 1), (3, 3))],
        6: [lambda: arrivals((2, 1), (2, 3))],
        8: [lambda: arrivals((1, 2), (3, 2)), lambda: far(0)],
        10: [lambda: near(0, 0)],
        11: [lambda: arrivals((2, 2))],
        12: [lambda: far(1)],
        14: [lambda: near(1, 0), lambda: near(1, 1), lambda: far(3)],
        15: [lambda: far(2)],
    }

    def send_back(k, index):
        return to(dev(0, 0, 1), terms1.at[index], back.at[k], back_s.at[k], back_r.at[k])

    all_grads = (grads0, grads1)
    grads1[...] = jnp.zeros_like(grads1)

    def step(j, _):
        for i in range(2):
            k = j * 2 + i
            for when, todo in acts.items():
                if when % 2 != i:
                    continue

                @pl.when(j == when // 2)
                def _():
                    for act in todo:
                        act()

            to(dev(0, 0, 1), sib.at[k], sib.at[k], sib_s.at[k], sib_r.at[k]).wait_recv()
            to(dev(0, 0, 1), pay.at[1, k], pay.at[1, k], pay_s.at[16 + k], pay_r.at[16 + k]).wait_recv()

            def mine():
                to(dev(0, 0, 1), pay.at[0, k], pay.at[0, k], pay_s.at[k], pay_r.at[k]).wait_recv()

            if i == 0:
                pl.when(j > 0)(mine)
            else:
                mine()

            last = lax.rem(k + 3, 4)

            @pl.when(k >= 5)
            def _():
                send_back(k - 5, last).wait_send()

            make_grads(k, own, sib, pay, w, all_grads[i], g_all, ids_all, loss_out)
            make_terms(k - 1 + lax.div(16 - k, 16), pay, w, all_grads[1 - i], terms0, terms1, last)

            def give():
                send_back(k - 1, last).start()

            if i == 0:
                pl.when(j > 0)(give)
            else:
                give()
        return 0

    lax.fori_loop(0, 8, step, 0)
    send_back(11, 3).wait_send()
    make_terms(15, pay, w, grads1, terms0, terms1, 3)
    send_back(15, 3).start()

    def shard(dx):
        weight_shard(lax.rem(mx + dx, 4) * 4, 4, sib, g_all, ids_all, wide, total)
        for h in (0, 1):
            shards_x[dx, h] = total[h * 256 : h * 256 + 256, :].astype(BF)

    def x_send(dx, h, part, store, sem):
        go(lambda: to_x(dx, shards_x.at[part, h], store(), x_s.at[sem], x_r.at[sem]))

    def x_wait(store, sem):
        to_x(1, store, store, x_s.at[sem], x_r.at[sem]).wait_recv()

    shard(2)
    x_send(1, 0, 2, lambda: half_x.at[0], 0)
    x_send(3, 1, 2, lambda: half_x.at[1], 1)
    near(2, 0)
    near(2, 1)
    near(3, 0)
    near(3, 1)
    near(0, 1)
    for k, (a, b) in enumerate(ORDER):
        for c in (0, 1):
            if k == 0 and c == 0:
                continue
            there = slot(-a, -b) if c == 0 else slot(-b, -a)
            go(
                lambda a=a, b=b, c=c, k=k, there=there: to(
                    dev(a, b, c), loss_out.at[c, k], loss_in.at[c, there],
                    loss_s.at[c * 16 + k], loss_r.at[c * 16 + there],
                )
            )
    here(2)
    halves_of(terms0, slot(2, 0), True, lambda h: half_a.at[h], 16)
    shard(1)
    x_send(1, 1, 1, lambda: full_x.at[0, 1], 3)
    here(1)
    here(3)
    meet(0, slot(1, 0), lambda h: half_a.at[h], 16)
    full_of(0, slot(1, 0), True, lambda h: full_a.at[h], 16)
    meet(1, slot(3, 0), lambda h: half_a.at[h], 16)
    full_of(1, slot(3, 0), True, lambda h: full_a.at[h], 16)
    shard(3)
    x_send(3, 0, 3, lambda: full_x.at[1, 0], 4)
    x_wait(half_x.at[0], 0)
    shards_x[1, 0] = shards_x[1, 0] + half_x[0]
    x_send(1, 0, 1, lambda: full_x.at[0, 0], 2)
    x_wait(half_x.at[1], 1)
    shards_x[3, 1] = shards_x[3, 1] + half_x[1]
    x_send(3, 1, 3, lambda: full_x.at[1, 1], 5)
    weight_shard(mx * 4, 4, sib, g_all, ids_all, wide, total)
    here(0)
    loss = loss_out[0, 0]
    for k in range(16):
        for c in (0, 1):
            if k == 0 and c == 0:
                continue
            ref = loss_in.at[c, k]
            to(dev(0, 0, 1), ref, ref, loss_s.at[c * 16 + k], loss_r.at[c * 16 + k]).wait_recv()
            loss = loss + loss_in[c, k]
    loss_ref[...] = loss[0:1, :]

    for h in (0, 1):
        got(lambda h: full_a.at[h], h, 18 + h)
    feat_ref[...] = terms0[0].astype(F32) + full_a[0].astype(F32) + full_a[1].astype(F32)

    for d in (0, 1):
        for h in (0, 1):
            x_wait(full_x.at[d, h], 2 + d * 2 + h)
    for h in (0, 1):
        weight_ref[h * 256 : h * 256 + 256, :] = (
            total[h * 256 : h * 256 + 256, :] + full_x[0, h].astype(F32) + full_x[1, h].astype(F32)
        ).astype(BF)

    for k in range(12, 16):
        send_back(k, k % 4).wait_send()
    for make in sent:
        make().wait_send()


def shards(queries_in, classifier, owner_ids, local_ids, targets):
    rows, width = queries_in.shape
    top = owner_ids.shape[1]
    pairs = rows * top
    vmem = pl.BlockSpec(memory_space=pltpu.VMEM)
    block = (rows, width)
    loss, feat, weight = pl.pallas_call(
        kernel,
        out_shape=(
            jax.ShapeDtypeStruct((1, rows), F32),
            jax.ShapeDtypeStruct(block, F32),
            jax.ShapeDtypeStruct((512, width), BF),
        ),
        in_specs=[vmem] * 5,
        out_specs=(vmem, vmem, vmem),
        scratch_shapes=[
            pltpu.VMEM((16, *block), BF),
            pltpu.VMEM((16, *block), BF),
            pltpu.VMEM((32, PAY, 128), BF),
            pltpu.VMEM((2, 16, PAY, 128), BF),
            pltpu.VMEM((16, *block), BF),
            pltpu.VMEM((4, *block), BF),
            pltpu.VMEM((16, *block), BF),
            pltpu.VMEM((4, 2, 128, width), BF),
            pltpu.VMEM((4, 2, *block), BF),
            pltpu.VMEM((2, 128, width), BF),
            pltpu.VMEM((2, *block), BF),
            pltpu.VMEM((512, width), F32),
            pltpu.VMEM((2, 256, width), BF),
            pltpu.VMEM((2, 2, 256, width), BF),
            pltpu.VMEM((4, 2, 256, width), BF),
            pltpu.VMEM((512, 1024), BF),
            pltpu.VMEM((16, 128, 256), BF),
            pltpu.VMEM((16, 16, 256), F32),
            *[pltpu.VMEM((2048, 256), BF)] * 2,
            pltpu.VMEM((2, 16, 8, rows), F32),
            pltpu.VMEM((2, 16, 8, rows), F32),
            pltpu.VMEM((pairs, 256), BF),
            pltpu.VMEM((32, rows), F32),
            pltpu.SemaphoreType.DMA((64,)),
            pltpu.SemaphoreType.DMA((32,)),
            pltpu.SemaphoreType.DMA((16,)),
            pltpu.SemaphoreType.DMA((16,)),
            pltpu.SemaphoreType.DMA((32,)),
            pltpu.SemaphoreType.DMA((32,)),
            pltpu.SemaphoreType.DMA((16,)),
            pltpu.SemaphoreType.DMA((16,)),
            pltpu.SemaphoreType.DMA((20,)),
            pltpu.SemaphoreType.DMA((20,)),
            pltpu.SemaphoreType.DMA((32,)),
            pltpu.SemaphoreType.DMA((32,)),
            pltpu.SemaphoreType.DMA((6,)),
            pltpu.SemaphoreType.DMA((6,)),
            pltpu.SemaphoreType.REGULAR((4,)),
        ],
        compiler_params=pltpu.CompilerParams(
            collective_id=0, has_side_effects=True, vmem_limit_bytes=64 * 1024 * 1024 - 65536
        ),
    )(
        queries_in, classifier, targets.reshape(pairs, 128), owner_ids.T, local_ids.T,
    )
    return loss.reshape(rows), feat, weight


def solution(mesh):
    in_specs = (
        P(("queries", "labels"), None),
        P("labels", None),
        P(("queries", "labels"), None),
        P(("queries", "labels"), None),
        P(("queries", "labels"), None, None),
    )
    out_specs = (
        P(("queries", "labels")),
        P(("queries", "labels"), None),
        P(("labels", "queries"), None),
    )
    return jax.shard_map(shards, mesh=mesh, in_specs=in_specs, out_specs=out_specs, check_vma=False)
```

time: 147 us -> 135 us (0.918)
  Pallas kernels: 138 us -> 128 us
  local copies, waits for them, and re-layouts: 8.35 us -> 5.36 us
    pallas_call x1, Pallas kernels: 138 us -> 128 us  [shards(): pl.pallas_call(kernel, out_shape=(jax.ShapeDtypeStruct((1, rows), F32), j...]
    unnamed x4 -> x3, local copies, waits for them, and re-layouts: 7.09 us -> 5.36 us
where the time goes in v3:
time: 135 us; the launch traced here: 134 us
  Pallas kernels  128 us (95%)
  local copies, waits for them, and re-layouts  5.36 us (4%)
    pallas_call x1, Pallas kernels, shards(): pl.pallas_call(kernel, out_shape=(jax.ShapeDtypeStruct((1, rows), F32), j...  128 us
    unnamed x3, local copies, waits for them, and re-layouts  5.36 us

profile of v3, /device:TPU:0, one launch (start us, length us, event | category | flops | bytes accessed | tf_op | source)
XLA Modules:
  0.0 134.2 jit_solution(17526859813447088250)
XLA Ops:
  0.6 128.2 %shard_map.76 = (f32[1,256]{1,0:T(1,128)}, f32[256,768]{1,0:T(8,128)}, bf16[512,768]{1,0:T(8,128)(2,1)}) custom-call(bf16[256,768]{1,0:T(8,128)(2,1)} %q_ref.1, bf16[2048,768]{1,0:T(8,128)(2,1)} %w.1, s32[2048,128]{1,0:T(8,128)} %bitcast.4, s32[8,256]{1,0:T(8,128)} %bitcast.5, s32[8,256]{1,0:T(8,128)} %bitcast.6), custom_call_target="tpu_custom_call" | custom-call | tf_op jit(solution)/shard_map/pallas_call | solution.py:502
  128.9 1.2 copy.11
  130.1 2.1 %copy.12 = f32[256,768]{1,0:T(8,128)} copy(f32[256,768]{1,0:T(8,128)} %get-tuple-element.13) | data formatting | bytes 1572864
  132.2 2.1 %copy.13 = bf16[512,768]{1,0:T(8,128)(2,1)} copy(bf16[512,768]{1,0:T(8,128)(2,1)} %get-tuple-element.14) | data formatting | bytes 1572864

commit v4 on v3

--- a/solution.py
+++ b/solution.py
@@ -42,7 +42,7 @@
     ).astype(BF)
 
 
-def make_grads(k, own, sib, pay, w, grads, g_all, ids_all, loss_out):
+def make_grads(k, own, sib, pay, w, grads, g_all, ids_all, loss_out, k1, grads1, terms0, terms1, index):
     picks = [pick_of(pay, core, k) for core in (0, 1)]
     x = jnp.concatenate(
         [nn(picks[core], src[k]).astype(BF) for core, src in enumerate((own, sib))], axis=0
@@ -52,13 +52,19 @@
         [pay[core, k, 128:144, :].astype(F32)[0:1, :] for core in (0, 1)], axis=1
     )
     z = jnp.zeros((128, 256), F32)
+    f = jnp.zeros((256, 768), F32)
     for part in range(2):
-        scores = nt(w[part * 1024 : part * 1024 + 1024, :], x)
+        at = slice(part * 1024, part * 1024 + 1024)
+        scores = nt(w[at, :], x)
+        f = f + tn(grads1[at, :], w[at, :])
         for b in range(8):
             z = jnp.where(ids == float(part * 8 + b + 1), scores[b * 128 : b * 128 + 128, :], z)
     z = z.astype(BF).astype(F32)
     y = jnp.concatenate([pay[core, k, 0:128, :] for core in (0, 1)], axis=1).astype(F32)
     valid = jnp.where(ids > 0.5, 0.25, 0.0)
+    f = f.astype(BF)
+    terms0[k1] = tn(pick_of(pay, 0, k1), f[0:128, :]).astype(BF)
+    terms1[index] = tn(pick_of(pay, 1, k1), f[128:256, :]).astype(BF)
     e = jnp.exp(-jnp.abs(z))
     loss = jnp.sum(jnp.maximum(z, 0.0) + jnp.log1p(e) - y * z, axis=0, keepdims=True) * valid
     sig = jnp.where(z >= 0.0, 1.0, e) / (1.0 + e)
@@ -87,22 +93,16 @@
     terms1[index] = tn(pick_of(pay, 1, k), f[128:256, :]).astype(BF)
 
 
-def weight_shard(first, count, sib, g_all, ids_all, wide, total):
-    def step(j, _):
-        for i in range(4):
-            k = j * 4 + i
-            many = ids_all[k]
-            g = g_all[k].reshape(8, 16, 256)
-            for b in range(count):
-                hot = jnp.where(many == (first + (b + 1)).astype(F32), 1.0, 0.0).astype(BF)
-                wide[b * 128 : b * 128 + 128, i * 256 : i * 256 + 256] = (g * hot[None]).reshape(128, 256)
-        size = count * 128
-        x = sib[pl.ds(j * 4, 4)].reshape(1024, 768)
-        total[0:size, :] += nn(wide[0:size, :], x)
-        return 0
-
-    total[...] = jnp.zeros_like(total)
-    lax.fori_loop(0, 4, step, 0)
+def weight_step(first, j, sib, g_all, ids_all, wide, total):
+    for i in range(4):
+        k = j * 4 + i
+        many = ids_all[k]
+        g = g_all[k].reshape(8, 16, 256)
+        for b in range(4):
+            hot = jnp.where(many == (first + (b + 1)).astype(F32), 1.0, 0.0).astype(BF)
+            wide[b * 128 : b * 128 + 128, i * 256 : i * 256 + 256] = (g * hot[None]).reshape(128, 256)
+    x = sib[pl.ds(j * 4, 4)].reshape(1024, 768)
+    total[...] += nn(wide[...], x)
 
 
 def kernel(
@@ -212,6 +212,7 @@
 
     own[0] = q_ref[...]
     pass_on(0)
+    total[...] = jnp.zeros_like(total)
 
     tell(0, ring_a)
     owners = owner_ref[...]
@@ -267,12 +268,13 @@
             pay_out[o, 128:144, :] = tail.astype(BF)
         return 0
 
-    lax.fori_loop(0, 4, pack, 0)
+    lax.fori_loop(0, 3, pack, 0)
     hear(1, 2)
     tell(2, ring_b)
-    lax.fori_loop(4, 8, pack, 0)
+    lax.fori_loop(3, 6, pack, 0)
     hear(2, 2)
     tell(3, (dev(0, 0, 1),))
+    lax.fori_loop(6, 8, pack, 0)
     hear(3, 1)
     pay[0, 0] = pay_out[me]
 
@@ -369,6 +371,9 @@
     all_grads = (grads0, grads1)
     grads1[...] = jnp.zeros_like(grads1)
 
+    def weights(dx, j):
+        weight_step(lax.rem(mx + dx, 4) * 4, j, sib, g_all, ids_all, wide, total.at[dx])
+
     def step(j, _):
         for i in range(2):
             k = j * 2 + i
@@ -398,8 +403,10 @@
             def _():
                 send_back(k - 5, last).wait_send()
 
-            make_grads(k, own, sib, pay, w, all_grads[i], g_all, ids_all, loss_out)
-            make_terms(k - 1 + lax.div(16 - k, 16), pay, w, all_grads[1 - i], terms0, terms1, last)
+            make_grads(
+                k, own, sib, pay, w, all_grads[i], g_all, ids_all, loss_out,
+                k - 1 + lax.div(16 - k, 16), all_grads[1 - i], terms0, terms1, last,
+            )
 
             def give():
                 send_back(k - 1, last).start()
@@ -408,6 +415,11 @@
                 pl.when(j > 0)(give)
             else:
                 give()
+
+            @pl.when(k >= 4)
+            def _():
+                weights(lax.rem(k, 4), k // 4 - 1)
+
         return 0
 
     lax.fori_loop(0, 8, step, 0)
@@ -416,9 +428,9 @@
     send_back(15, 3).start()
 
     def shard(dx):
-        weight_shard(lax.rem(mx + dx, 4) * 4, 4, sib, g_all, ids_all, wide, total)
+        weights(dx, 3)
         for h in (0, 1):
-            shards_x[dx, h] = total[h * 256 : h * 256 + 256, :].astype(BF)
+            shards_x[dx, h] = total[dx, h * 256 : h * 256 + 256, :].astype(BF)
 
     def x_send(dx, h, part, store, sem):
         go(lambda: to_x(dx, shards_x.at[part, h], store(), x_s.at[sem], x_r.at[sem]))
@@ -434,6 +446,10 @@
     near(3, 0)
     near(3, 1)
     near(0, 1)
+    shard(1)
+    x_send(1, 1, 1, lambda: full_x.at[0, 1], 3)
+    shard(3)
+    x_send(3, 0, 3, lambda: full_x.at[1, 0], 4)
     for k, (a, b) in enumerate(ORDER):
         for c in (0, 1):
             if k == 0 and c == 0:
@@ -447,23 +463,19 @@
             )
     here(2)
     halves_of(terms0, slot(2, 0), True, lambda h: half_a.at[h], 16)
-    shard(1)
-    x_send(1, 1, 1, lambda: full_x.at[0, 1], 3)
     here(1)
-    here(3)
-    meet(0, slot(1, 0), lambda h: half_a.at[h], 16)
-    full_of(0, slot(1, 0), True, lambda h: full_a.at[h], 16)
-    meet(1, slot(3, 0), lambda h: half_a.at[h], 16)
-    full_of(1, slot(3, 0), True, lambda h: full_a.at[h], 16)
-    shard(3)
-    x_send(3, 0, 3, lambda: full_x.at[1, 0], 4)
     x_wait(half_x.at[0], 0)
     shards_x[1, 0] = shards_x[1, 0] + half_x[0]
     x_send(1, 0, 1, lambda: full_x.at[0, 0], 2)
     x_wait(half_x.at[1], 1)
     shards_x[3, 1] = shards_x[3, 1] + half_x[1]
     x_send(3, 1, 3, lambda: full_x.at[1, 1], 5)
-    weight_shard(mx * 4, 4, sib, g_all, ids_all, wide, total)
+    meet(0, slot(1, 0), lambda h: half_a.at[h], 16)
+    full_of(0, slot(1, 0), True, lambda h: full_a.at[h], 16)
+    here(3)
+    meet(1, slot(3, 0), lambda h: half_a.at[h], 16)
+    full_of(1, slot(3, 0), True, lambda h: full_a.at[h], 16)
+    weights(0, 3)
     here(0)
     loss = loss_out[0, 0]
     for k in range(16):
@@ -484,7 +496,7 @@
             x_wait(full_x.at[d, h], 2 + d * 2 + h)
     for h in (0, 1):
         weight_ref[h * 256 : h * 256 + 256, :] = (
-            total[h * 256 : h * 256 + 256, :] + full_x[0, h].astype(F32) + full_x[1, h].astype(F32)
+            total[0, h * 256 : h * 256 + 256, :] + full_x[0, h].astype(F32) + full_x[1, h].astype(F32)
         ).astype(BF)
 
     for k in range(12, 16):
@@ -520,7 +532,7 @@
             pltpu.VMEM((4, 2, *block), BF),
             pltpu.VMEM((2, 128, width), BF),
             pltpu.VMEM((2, *block), BF),
-            pltpu.VMEM((512, width), F32),
+            pltpu.VMEM((4, 512, width), F32),
             pltpu.VMEM((2, 256, width), BF),
             pltpu.VMEM((2, 2, 256, width), BF),
             pltpu.VMEM((4, 2, 256, width), BF),

time: 135 us -> 130 us (0.963)
  Pallas kernels: 128 us -> 122 us
    pallas_call x1, Pallas kernels: 128 us -> 122 us  [shards(): pl.pallas_call(kernel, out_shape=(jax.ShapeDtypeStruct((1, rows), F32), j...]
where the time goes in v4:
time: 130 us; the launch traced here: 128 us
  Pallas kernels  122 us (94%)
  local copies, waits for them, and re-layouts  5.36 us (4%)
    pallas_call x1, Pallas kernels, shards(): pl.pallas_call(kernel, out_shape=(jax.ShapeDtypeStruct((1, rows), F32), j...  122 us
    unnamed x3, local copies, waits for them, and re-layouts  5.36 us

profile of v4, /device:TPU:0, one launch (start us, length us, event | category | flops | bytes accessed | tf_op | source)
XLA Modules:
  0.0 128.4 jit_solution(15636312029658124545)
XLA Ops:
  0.6 122.4 %shard_map.76 = (f32[1,256]{1,0:T(1,128)}, f32[256,768]{1,0:T(8,128)}, bf16[512,768]{1,0:T(8,128)(2,1)}) custom-call(bf16[256,768]{1,0:T(8,128)(2,1)} %q_ref.1, bf16[2048,768]{1,0:T(8,128)(2,1)} %w.1, s32[2048,128]{1,0:T(8,128)} %bitcast.4, s32[8,256]{1,0:T(8,128)} %bitcast.5, s32[8,256]{1,0:T(8,128)} %bitcast.6), custom_call_target="tpu_custom_call" | custom-call | tf_op jit(solution)/shard_map/pallas_call | solution.py:514
  123.1 1.2 copy.11
  124.3 2.1 %copy.12 = f32[256,768]{1,0:T(8,128)} copy(f32[256,768]{1,0:T(8,128)} %get-tuple-element.13) | data formatting | bytes 1572864
  126.4 2.1 %copy.13 = bf16[512,768]{1,0:T(8,128)(2,1)} copy(bf16[512,768]{1,0:T(8,128)(2,1)} %get-tuple-element.14) | data formatting | bytes 1572864

commit v5 on v4

--- a/solution.py
+++ b/solution.py
@@ -11,7 +11,7 @@
 
 ORDER = [
     (0, 0), (0, 1), (1, 0), (0, 2), (2, 0), (1, 1), (1, 3), (3, 1),
-    (3, 3), (2, 1), (1, 2), (2, 3), (3, 2), (2, 2), (0, 3), (3, 0),
+    (3, 3), (2, 1), (1, 2), (2, 2), (2, 3), (3, 2), (0, 3), (3, 0),
 ]
 SLOT = {chip: k for k, chip in enumerate(ORDER)}
 MIRROR = [SLOT[(b, a)] for a, b in ORDER]
@@ -358,11 +358,11 @@
         4: [lambda: targets_to(range(13, 16)), lambda: arrivals((1, 1), (1, 3), (3, 1), (3, 3))],
         6: [lambda: arrivals((2, 1), (2, 3))],
         8: [lambda: arrivals((1, 2), (3, 2)), lambda: far(0)],
-        10: [lambda: near(0, 0)],
-        11: [lambda: arrivals((2, 2))],
+        10: [lambda: near(0, 0), lambda: arrivals((2, 2))],
         12: [lambda: far(1)],
-        14: [lambda: near(1, 0), lambda: near(1, 1), lambda: far(3)],
-        15: [lambda: far(2)],
+        13: [lambda: far(2)],
+        14: [lambda: near(1, 0), lambda: near(1, 1)],
+        15: [lambda: near(2, 0), lambda: far(3)],
     }
 
     def send_back(k, index):
@@ -423,9 +423,6 @@
         return 0
 
     lax.fori_loop(0, 8, step, 0)
-    send_back(11, 3).wait_send()
-    make_terms(15, pay, w, grads1, terms0, terms1, 3)
-    send_back(15, 3).start()
 
     def shard(dx):
         weights(dx, 3)
@@ -441,7 +438,9 @@
     shard(2)
     x_send(1, 0, 2, lambda: half_x.at[0], 0)
     x_send(3, 1, 2, lambda: half_x.at[1], 1)
-    near(2, 0)
+    send_back(11, 3).wait_send()
+    make_terms(15, pay, w, grads1, terms0, terms1, 3)
+    send_back(15, 3).start()
     near(2, 1)
     near(3, 0)
     near(3, 1)

time: 130 us -> 127 us (0.977)
  Pallas kernels: 122 us -> 120 us
    pallas_call x1, Pallas kernels: 122 us -> 120 us  [shards(): pl.pallas_call(kernel, out_shape=(jax.ShapeDtypeStruct((1, rows), F32), j...]
where the time goes in v5:
time: 127 us; the launch traced here: 126 us
  Pallas kernels  120 us (94%)
  local copies, waits for them, and re-layouts  5.36 us (4%)
    pallas_call x1, Pallas kernels, shards(): pl.pallas_call(kernel, out_shape=(jax.ShapeDtypeStruct((1, rows), F32), j...  120 us
    unnamed x3, local copies, waits for them, and re-layouts  5.36 us

profile of v5, /device:TPU:0, one launch (start us, length us, event | category | flops | bytes accessed | tf_op | source)
XLA Modules:
  0.0 126.0 jit_solution(7901516650208113556)
XLA Ops:
  0.6 120.0 %shard_map.76 = (f32[1,256]{1,0:T(1,128)}, f32[256,768]{1,0:T(8,128)}, bf16[512,768]{1,0:T(8,128)(2,1)}) custom-call(bf16[256,768]{1,0:T(8,128)(2,1)} %q_ref.1, bf16[2048,768]{1,0:T(8,128)(2,1)} %w.1, s32[2048,128]{1,0:T(8,128)} %bitcast.4, s32[8,256]{1,0:T(8,128)} %bitcast.5, s32[8,256]{1,0:T(8,128)} %bitcast.6), custom_call_target="tpu_custom_call" | custom-call | tf_op jit(solution)/shard_map/pallas_call | solution.py:513
  120.6 1.2 copy.11
  121.9 2.1 %copy.12 = f32[256,768]{1,0:T(8,128)} copy(f32[256,768]{1,0:T(8,128)} %get-tuple-element.13) | data formatting | bytes 1572864
  123.9 2.1 %copy.13 = bf16[512,768]{1,0:T(8,128)(2,1)} copy(bf16[512,768]{1,0:T(8,128)(2,1)} %get-tuple-element.14) | data formatting | bytes 1572864
